TPU v7x, 128 devices: a whole 4x4x4 slice. The times are simulated.
128 devices in a mesh: cols: 8 (over z, core), depth: 16 (over x, y).
Axes of the slice: x: 4, y: 4, z: 4, core: 2. Of those that a mesh axis runs over, the one named last changes fastest.
Arguments:
- qtensor: bfloat16 [5, 128, 128, 1024], P(None, 'depth', None, 'cols'), may hold values from -2.5 to 2.5
- labels: int32 [128, 128, 1024], P('depth', None, 'cols'), may hold values from 0 to 3
- tables: float32 [4, 4, 16], replicated, may hold values from 0.2 to 2
Outputs:
- image: float32 [4, 128, 1024], P(None, 'depth', 'cols')
All inputs are finite; a program needn't handle non-finite values.
Results may differ from a plain program's by a relative error of at most 0.0003.
Values may be sent and summed in bfloat16 or wider, within the bound.
No kernel may reach another device: no remote copies, remote signals or barrier semaphores. Data moves between devices by JAX's collectives and lax.ppermute only.
A program may use at most 64 MiB of HBM per device.

v0:
```python
import jax
import jax.numpy as jnp
from jax import lax
from jax.sharding import PartitionSpec as P


def with_halo(array, sides, width):
    for axis, dim in sides:
        peers, length = (lax.axis_size(axis), array.shape[dim])
        up = [(i, (i + 1) % peers) for i in range(peers - 1)]
        down = [(j, i) for i, j in up]
        last = lax.slice_in_dim(array, length - width, length, axis=dim)
        initial = lax.slice_in_dim(array, 0, width, axis=dim)
        before = lax.ppermute(last, axis, up)
        after = lax.ppermute(initial, axis, down)
        array = jnp.concatenate([before, array, after], axis=dim)
    return array


def from_partner(block, axis, bit):
    count = lax.axis_size(axis)
    route = []
    for low in range(count):
        high = low | 1 << bit
        if high != low and high < count:
            route += [(low, high), (high, low)]
    return lax.ppermute(block, axis, route)


def strength_of(q):
    q = q.astype(jnp.float32)
    return 3.0 * (q[0] * q[0] + q[3] * q[3] + q[0] * q[3] + q[1] * q[1] + q[2] * q[2] + q[4] * q[4])


def slope_of(padded):
    dz = (padded[2:, 1:-1, 1:-1] - padded[:-2, 1:-1, 1:-1]) * 0.5
    dy = (padded[1:-1, 2:, 1:-1] - padded[1:-1, :-2, 1:-1]) * 0.5
    dx = (padded[1:-1, 1:-1, 2:] - padded[1:-1, 1:-1, :-2]) * 0.5
    return dz * dz + dy * dy + dx * dx


def shade(strength, slope, labels, tables, step):
    nbins = tables.shape[2]
    nlab = tables.shape[0]
    coord = jnp.clip(2.0 * strength, 0.0, nbins - 1.0)
    masks = [(labels == lab).astype(jnp.float32) for lab in range(nlab)]
    values = [jnp.zeros_like(strength) for chan in range(4)]
    for knot in range(nbins):
        weight = jnp.maximum(0.0, 1.0 - jnp.abs(coord - knot))
        for chan in range(4):
            picked = masks[0] * tables[0, chan, knot]
            for lab in range(1, nlab):
                picked = picked + masks[lab] * tables[lab, chan, knot]
            values[chan] = values[chan] + weight * picked
    extinction = values[3] * (0.25 + slope / (1.0 + slope))
    alpha = 1.0 - jnp.exp(-step * extinction)
    before = jnp.cumsum(extinction, axis=0) - extinction
    transmit = jnp.exp(-step * before)
    weighted = transmit * alpha
    colors = [jnp.sum(weighted * values[chan], axis=0) for chan in range(3)]
    opacity = 1.0 - jnp.exp(-step * jnp.sum(extinction, axis=0))
    return jnp.stack(colors + [opacity], axis=0)


def over(front, back):
    cover = 1.0 - front[3:4]
    return front + cover * back


def on_device(qtensor, labels, tables):
    depth_dev = qtensor.shape[1]
    rows_all = qtensor.shape[2]
    groups = lax.axis_size("depth")
    step = 2.0 / (depth_dev * groups)
    strength = strength_of(qtensor)
    wide = with_halo(strength, (("cols", 2), ("depth", 0)), 1)
    strength_in = wide[1:-1, :, 1:-1]
    padded = jnp.pad(wide, ((0, 0), (1, 1), (0, 0)))
    partial_img = shade(strength_in, slope_of(padded), labels, tables, step)
    block = rows_all // groups
    pieces = partial_img.reshape(4, groups, block, partial_img.shape[2])
    mine = lax.axis_index("depth")
    levels = groups.bit_length() - 1
    current = pieces
    for bit in range(levels):
        upper = mine >> bit & 1 == 1
        even = current[:, 0::2]
        odd = current[:, 1::2]
        keep = jnp.where(upper, odd, even)
        give = jnp.where(upper, even, odd)
        came = from_partner(give, "depth", bit)
        front = jnp.where(upper, came, keep)
        back = jnp.where(upper, keep, came)
        current = over(front, back)
    return current.reshape(4, block, partial_img.shape[2])


def solution(mesh):
    placed = (P(None, "depth", None, "cols"), P("depth", None, "cols"), P())
    return jax.shard_map(
        on_device, mesh=mesh, in_specs=placed, out_specs=P(None, "depth", "cols"), check_vma=False
    )
```

profile of v0, /device:TPU:38, one launch (start us, length us, event | category | flops | bytes accessed | tf_op | source)
XLA Modules:
  0.0 230.9 jit_solution(2400673082569445213)
XLA Ops:
  0.0 1.6 convert_element_type.4
  2.1 1.9 collective-permute-start
  4.0 3.6 %collective-permute-start.1 = (f32[8,128,1]{2,1,0:T(8,128)S(1)}, f32[8,128,1]{2,1,0:T(8,128)S(1)}, u32[]{:S(2)}, u32[]{:S(2)}) collective-permute-start(f32[8,128,1]{2,1,0:T(8,128)S(1)} %get-tuple-element.15), channel_id=1, source_target_pairs={{16,0},{32,16},{48,32},{64,48},{80,64},{96,80},{112,96},{17,1},{33... | collective-permute-start | bytes 12296 | tf_op jit(solution)/shard_map/ppermute | solution.py:15
  7.7 0.7 fusion.105
  8.4 0.7 fusion.104
  9.1 0.7 fusion.96
  9.8 0.7 fusion.106
  10.5 0.7 fusion.100
  11.2 0.7 fusion.99
  12.0 0.7 fusion.98
  12.7 0.7 fusion.97
  13.4 0.7 fusion.95
  14.2 0.7 fusion.94
  14.9 0.7 fusion.93
  15.6 0.7 fusion.101
  16.3 0.7 fusion.102
  17.3 5.2 %collective-permute-start.2 = (f32[1,128,130]{2,1,0:T(8,128)S(1)}, f32[1,128,130]{2,1,0:T(8,128)S(1)}, u32[]{:S(2)}, u32[]{:S(2)}) collective-permute-start(f32[1,128,130]{2,1,0:T(8,128)S(1)} %get-tuple-element.14), channel_id=1, source_target_pairs={{1,0},{2,1},{3,2},{4,3},{5,4},{6,5},{7,6},{8,7},{9,8},{10,9},{11,1... | collective-permute-start | bytes 199688 | tf_op jit(solution)/shard_map/ppermute | solution.py:15
  22.5 1.9 collective-permute-start.3
  24.4 0.7 fusion.103
  25.1 0.6 collective-permute-done.2
  25.7 6.2 %collective-permute-done.3 = f32[1,128,130]{2,1,0:T(8,128)S(1)} collective-permute-done((f32[1,128,130]{2,1,0:T(8,128)S(1)}, f32[1,128,130]{2,1,0:T(8,128)S(1)}, u32[]{:S(2)}, u32[]{:S(2)}) %collective-permute-start.3) | collective-permute-done | bytes 66592 | tf_op jit(solution)/shard_map/ppermute | solution.py:14
  32.4 44.8 %fusion.89 = (f32[128,128]{1,0:T(8,128)S(1)}, f32[8,128,128]{2,1,0:T(8,128)S(1)}, pred[8,128,128]{2,1,0:T(8,128)(4,1)S(1)}, pred[8,128,128]{2,1,0:T(8,128)(4,1)S...) fusion(f32[8,128,128]{2,1,0:T(8,128)S(1)} %get-tuple-element.11, ...), kind=kLoop, calls=%fused_computation.220 | loop fusion | flops 30916608 | bytes 3877120 | tf_op jit(solution)/shard_map/reduce_sum | solution.py:61
  77.2 44.1 %fusion.28 = (f32[128,128]{1,0:T(8,128)S(1)}, f32[8,128,128]{2,1,0:T(8,128)S(1)}) fusion(pred[8,128,128]{2,1,0:T(8,128)(4,1)S(1)} %get-tuple-element.10, pred[8,128,128]{2,1,0:T(8,128)(4,1)S(1)} %get-tuple-element.9, pred[8,128,128]{2,1,0:T(8,128)(4,1)S(1)} %get-tuple-element.8, pred[8,128,128]{2,1,0:T(8,128)(4,1)S(1)} %get-tuple-element.7, f32[]{:T(128)} %bitcast.274, ...), kind=kOutput, calls=%fused_computation.52 | output fusion | flops 29081600 | bytes 2162944 | tf_op jit(solution)/shard_map/jit(cumsum)/reduce_window_sum | solution.py:57
  121.4 43.9 %fusion.22 = f32[128,128]{1,0:T(8,128)S(1)} fusion(f32[8,128,128]{2,1,0:T(8,128)S(1)} %get-tuple-element.274, pred[8,128,128]{2,1,0:T(8,128)(4,1)S(1)} %get-tuple-element.10, pred[8,128,128]{2,1,0:T(8,128)(4,1)S(1)} %get-tuple-element.9, pred[8,128,128]{2,1,0:T(8,128)(4,1)S(1)} %get-tuple-element.8, pred[8,128,128]{2,1,0:T(8,128)(4,1)S(1)} %get-tuple-element.7, ...), kind=kLoop, calls=%fused_computation.46 | loop fusion | flops 27508736 | bytes 1638656 | tf_op jit(solution)/shard_map/reduce_sum | solution.py:60
  165.2 43.9 %fusion.25 = f32[128,128]{1,0:T(8,128)S(1)} fusion(f32[8,128,128]{2,1,0:T(8,128)S(1)} %get-tuple-element.274, pred[8,128,128]{2,1,0:T(8,128)(4,1)S(1)} %get-tuple-element.10, pred[8,128,128]{2,1,0:T(8,128)(4,1)S(1)} %get-tuple-element.9, pred[8,128,128]{2,1,0:T(8,128)(4,1)S(1)} %get-tuple-element.8, pred[8,128,128]{2,1,0:T(8,128)(4,1)S(1)} %get-tuple-element.7, ...), kind=kLoop, calls=%fused_computation.49 | loop fusion | flops 27508736 | bytes 1638656 | tf_op jit(solution)/shard_map/reduce_sum | solution.py:60
  209.3 5.6 %collective-permute-done.4 = f32[4,8,8,128]{3,2,0,1:T(8,128)S(1)} collective-permute-done((f32[4,8,8,128]{3,2,0,1:T(8,128)S(1)}, f32[4,8,8,128]{3,2,0,1:T(8,128)S(1)}, u32[]{:S(2)}, u32[]{:S(2)}) %collective-permute-start.4) | collective-permute-done | bytes 131104 | tf_op jit(solution)/shard_map/ppermute | solution.py:27
  215.1 5.8 %collective-permute-done.5 = f32[4,4,8,128]{3,2,0,1:T(8,128)S(1)} collective-permute-done((f32[4,4,8,128]{3,2,0,1:T(8,128)S(1)}, f32[4,4,8,128]{3,2,0,1:T(8,128)S(1)}, u32[]{:S(2)}, u32[]{:S(2)}) %collective-permute-start.5) | collective-permute-done | bytes 65568 | tf_op jit(solution)/shard_map/ppermute | solution.py:27
  220.9 0.6 collective-permute-start.6
  221.6 3.4 %collective-permute-done.6 = f32[4,2,8,128]{3,2,0,1:T(8,128)S(1)} collective-permute-done((f32[4,2,8,128]{3,2,0,1:T(8,128)S(1)}, f32[4,2,8,128]{3,2,0,1:T(8,128)S(1)}, u32[]{:S(2)}, u32[]{:S(2)}) %collective-permute-start.6) | collective-permute-done | bytes 32800 | tf_op jit(solution)/shard_map/ppermute | solution.py:27
  225.0 1.3 collective-permute-start.7
  226.3 4.0 %collective-permute-done.7 = f32[4,1,8,128]{3,2,0,1:T(8,128)S(1)} collective-permute-done((f32[4,1,8,128]{3,2,0,1:T(8,128)S(1)}, f32[4,1,8,128]{3,2,0,1:T(8,128)S(1)}, u32[]{:S(2)}, u32[]{:S(2)}) %collective-permute-start.7) | collective-permute-done | bytes 16416 | tf_op jit(solution)/shard_map/ppermute | solution.py:27
  230.3 0.6 add_bitcast_fusion
  (29 shorter events, 1.5 us)
Async XLA Ops:
  1.9 5.8 %copy-start = (f32[4,4,16]{2,1,0:T(4,128)S(1)}, f32[4,4,16]{2,1,0:T(4,128)}, u32[]{:S(2)}) copy-start(f32[4,4,16]{2,1,0:T(4,128)} %param.5) | copy-start | bytes 3076
  2.1 15.0 %collective-permute-start = (f32[8,128,1]{2,1,0:T(8,128)S(1)}, f32[8,128,1]{2,1,0:T(8,128)S(1)}, u32[]{:S(2)}, u32[]{:S(2)}) collective-permute-start(f32[8,128,1]{2,1,0:T(8,128)S(1)} %get-tuple-element.16), channel_id=1, source_target_pairs={{0,16},{16,32},{32,48},{48,64},{64,80},{80,96},{96,112},{1,17},{17... | collective-permute-start | bytes 12296 | tf_op jit(solution)/shard_map/ppermute | solution.py:14
  4.0 13.1 %collective-permute-start.1 = (f32[8,128,1]{2,1,0:T(8,128)S(1)}, f32[8,128,1]{2,1,0:T(8,128)S(1)}, u32[]{:S(2)}, u32[]{:S(2)}) collective-permute-start(f32[8,128,1]{2,1,0:T(8,128)S(1)} %get-tuple-element.15), channel_id=1, source_target_pairs={{16,0},{32,16},{48,32},{64,48},{80,64},{96,80},{112,96},{17,1},{33... | collective-permute-start | bytes 12296 | tf_op jit(solution)/shard_map/ppermute | solution.py:15
  17.3 8.4 %collective-permute-start.2 = (f32[1,128,130]{2,1,0:T(8,128)S(1)}, f32[1,128,130]{2,1,0:T(8,128)S(1)}, u32[]{:S(2)}, u32[]{:S(2)}) collective-permute-start(f32[1,128,130]{2,1,0:T(8,128)S(1)} %get-tuple-element.14), channel_id=1, source_target_pairs={{1,0},{2,1},{3,2},{4,3},{5,4},{6,5},{7,6},{8,7},{9,8},{10,9},{11,1... | collective-permute-start | bytes 199688 | tf_op jit(solution)/shard_map/ppermute | solution.py:15
  22.5 9.4 %collective-permute-start.3 = (f32[1,128,130]{2,1,0:T(8,128)S(1)}, f32[1,128,130]{2,1,0:T(8,128)S(1)}, u32[]{:S(2)}, u32[]{:S(2)}) collective-permute-start(f32[1,128,130]{2,1,0:T(8,128)S(1)} %get-tuple-element.13), channel_id=1, source_target_pairs={{0,1},{1,2},{2,3},{3,4},{4,5},{5,6},{6,7},{7,8},{8,9},{9,10},{10,1... | collective-permute-start | bytes 199688 | tf_op jit(solution)/shard_map/ppermute | solution.py:14
  25.1 7.3 %copy-start.1 = (s32[8,128,128]{2,1,0:T(8,128)S(1)}, s32[8,128,128]{2,1,0:T(8,128)}, u32[]{:S(2)}) copy-start(s32[8,128,128]{2,1,0:T(8,128)} %param.4) | copy-start | bytes 1572868
  209.2 5.7 %collective-permute-start.4 = (f32[4,8,8,128]{3,2,0,1:T(8,128)S(1)}, f32[4,8,8,128]{3,2,0,1:T(8,128)S(1)}, u32[]{:S(2)}, u32[]{:S(2)}) collective-permute-start(f32[4,8,8,128]{3,2,0,1:T(8,128)S(1)} %slice_select_fusion.1), channel_id=1, source_target_pairs={{0,1},{1,0},{2,3},{3,2},{4,5},{5,4},{6,7},{7,6},{8,9},{9,8},{10,11... | collective-permute-start | bytes 393224 | tf_op jit(solution)/shard_map/ppermute | solution.py:27
  215.0 5.8 %collective-permute-start.5 = (f32[4,4,8,128]{3,2,0,1:T(8,128)S(1)}, f32[4,4,8,128]{3,2,0,1:T(8,128)S(1)}, u32[]{:S(2)}, u32[]{:S(2)}) collective-permute-start(f32[4,4,8,128]{3,2,0,1:T(8,128)S(1)} %slice_select_fusion.3), channel_id=1, source_target_pairs={{0,2},{2,0},{1,3},{3,1},{4,6},{6,4},{5,7},{7,5},{8,10},{10,8},{9,1... | collective-permute-start | bytes 196616 | tf_op jit(solution)/shard_map/ppermute | solution.py:27
  220.9 4.0 %collective-permute-start.6 = (f32[4,2,8,128]{3,2,0,1:T(8,128)S(1)}, f32[4,2,8,128]{3,2,0,1:T(8,128)S(1)}, u32[]{:S(2)}, u32[]{:S(2)}) collective-permute-start(f32[4,2,8,128]{3,2,0,1:T(8,128)S(1)} %slice_select_fusion.5), channel_id=1, source_target_pairs={{0,4},{4,0},{1,5},{5,1},{2,6},{6,2},{3,7},{7,3},{8,12},{12,8},{9,1... | collective-permute-start | bytes 98312 | tf_op jit(solution)/shard_map/ppermute | solution.py:27
  225.0 5.3 %collective-permute-start.7 = (f32[4,1,8,128]{3,2,0,1:T(8,128)S(1)}, f32[4,1,8,128]{3,2,0,1:T(8,128)S(1)}, u32[]{:S(2)}, u32[]{:S(2)}) collective-permute-start(f32[4,1,8,128]{3,2,0,1:T(8,128)S(1)} %slice_select_fusion.7), channel_id=1, source_target_pairs={{0,8},{8,0},{1,9},{9,1},{2,10},{10,2},{3,11},{11,3},{4,12},{12,4},... | collective-permute-start | bytes 49160 | tf_op jit(solution)/shard_map/ppermute | solution.py:27
where the time goes:
time: 233 us; the launch traced here: 231 us
  other arithmetic  180 us (77%)
  waiting for transfers between devices  25.6 us (11%)
  starting transfers between devices  14.8 us (6%)
  local copies, waits for them, and re-layouts  10.3 us (4%)
    reduce_sum x2, other arithmetic, shade(): colors = [jnp.sum(weighted * values[chan], axis=0) for chan in range(3)]  87.7 us
    reduce_sum x1, other arithmetic, shade(): opacity = 1.0 - jnp.exp(-step * jnp.sum(extinction, axis=0))  44.8 us
    another operation x1, other arithmetic, shade(): before = jnp.cumsum(extinction, axis=0) - extinction  44.1 us
    ppermute x4, waiting for transfers between devices, from_partner(): return lax.ppermute(block, axis, route)  18.8 us
    ppermute x2, starting transfers between devices, with_halo(): after = lax.ppermute(initial, axis, down)  8.83 us
    slice x10, local copies, waits for them, and re-layouts, shade(): picked = picked + masks[lab] * tables[lab, chan, knot]  7.27 us
    ppermute x2, waiting for transfers between devices, with_halo(): before = lax.ppermute(last, axis, up)  6.23 us
  transfers between devices with their start and end apart: 8, of which 6 were waited for; matrix products, arithmetic and copies ran while one was open for 4% of the time, Pallas kernels for 0%

commit v1 on v0

v1 whole, which is shorter than its diff:
```python
import functools
import jax
import jax.numpy as jnp
from jax import lax
from jax.experimental import pallas as pl
from jax.experimental.pallas import tpu as pltpu
from jax.sharding import PartitionSpec as P

LANES = 128
SUB = 8
PAD = 8


def strength_kernel(q_ref, s_ref, first_ref, last_ref, colfirst_ref, collast_ref, edge, edge_t):
    _, nz, rows, lanes = q_ref.shape
    lane = lax.broadcasted_iota(jnp.int32, (16, lanes), 1)
    zeros = jnp.zeros((PAD, lanes), jnp.float32)
    for z in range(nz):
        s_ref[z, 0:PAD, :] = zeros
        s_ref[z, PAD + rows:, :] = zeros

    def block(i, carry):
        r0 = pl.multiple_of(i * 16, 16)
        packed = jnp.zeros((16, lanes), jnp.float32)
        for z in range(nz):
            q = [q_ref[c, z, pl.ds(r0, 16), :].astype(jnp.float32) for c in range(5)]
            s = 3.0 * (q[0] * q[0] + q[3] * q[3] + q[0] * q[3] + q[1] * q[1] + q[2] * q[2] + q[4] * q[4])
            s_ref[z, pl.ds(r0 + PAD, 16), :] = s
            if z == 0:
                first_ref[pl.ds(r0, 16), :] = s
            if z == nz - 1:
                last_ref[pl.ds(r0, 16), :] = s
            turned = pltpu.roll(s, 2 * z + 1, 1)
            packed = jnp.where(lane >> 1 == z, turned, packed)
        edge[pl.ds(r0, 16), :] = packed
        return carry

    lax.fori_loop(0, rows // 16, block, 0)
    edge_t[...] = edge[...].T
    collast_ref[...] = edge_t[pl.ds(0, nz, stride=2), :]
    colfirst_ref[...] = edge_t[pl.ds(1, nz, stride=2), :]


def shade_kernel(step, tab_ref, s_ref, lab_ref, before_ref, after_ref, left_ref, right_ref, out_ref, rows_tab, halo, halo_t):
    nz, rows, lanes = lab_ref.shape
    nlab, nchan, nbins = tab_ref.shape
    d = lax.axis_index("depth")
    c = lax.axis_index("cols")
    has_before = (d > 0).astype(jnp.float32)
    has_after = (d < lax.axis_size("depth") - 1).astype(jnp.float32)
    has_left = (c > 0).astype(jnp.float32)
    has_right = (c < lax.axis_size("cols") - 1).astype(jnp.float32)

    lane = lax.broadcasted_iota(jnp.int32, (SUB, lanes), 1)
    knots = jnp.zeros((SUB, lanes), jnp.float32)
    rows_tab[...] = jnp.zeros_like(rows_tab)
    for lab in range(nlab):
        rows_tab[lab, 0:nchan, 0:nbins] = tab_ref[lab]
    for lab in range(nlab):
        knots = knots + pltpu.roll(rows_tab[lab], lab * nbins, 1)
    delta = pltpu.roll(knots, lanes - 1, 1) - knots
    delta = jnp.where(lane < nlab * nbins, delta, 0.0)
    half = nlab * nbins
    both = knots + pltpu.roll(delta, half, 1)
    table = [jnp.broadcast_to(both[k:k + 1, :], (SUB, lanes)) for k in range(nchan)]

    halo[pl.ds(0, nz, stride=2), :] = left_ref[...] * has_left
    halo[pl.ds(1, nz, stride=2), :] = right_ref[...] * has_right
    halo_t[...] = halo[...].T

    def block(i, carry):
        r0 = pl.multiple_of(i * SUB, SUB)
        at = pl.ds(r0, SUB)
        sides = halo_t[at, :]
        transmit = jnp.ones((SUB, lanes), jnp.float32)
        colors = [jnp.zeros((SUB, lanes), jnp.float32) for _ in range(3)]
        below = before_ref[at, :] * has_before
        here = s_ref[0, pl.ds(r0 + PAD, SUB), :]
        for z in range(nz):
            if z == nz - 1:
                above = after_ref[at, :] * has_after
            else:
                above = s_ref[z + 1, pl.ds(r0 + PAD, SUB), :]
            side = pltpu.roll(sides, lanes - 1 - 2 * z, 1)
            to_left = pltpu.roll(jnp.where(lane == lanes - 1, side, here), 1, 1)
            to_right = pltpu.roll(jnp.where(lane == 0, side, here), lanes - 1, 1)
            dz = above - below
            dx = to_right - to_left
            dy = s_ref[z, pl.ds(r0 + PAD + 1, SUB), :] - s_ref[z, pl.ds(r0 + PAD - 1, SUB), :]
            slope = 0.25 * (dz * dz + dy * dy + dx * dx)
            coord = jnp.clip(2.0 * here, 0.0, nbins - 1.0)
            knot = coord.astype(jnp.int32)
            frac = coord - knot.astype(jnp.float32)
            index = lab_ref[z, at, :] * nbins + knot
            index2 = index + half
            value = []
            for chan in range(nchan):
                base = jnp.take_along_axis(table[chan], index, axis=1, mode="promise_in_bounds")
                diff = jnp.take_along_axis(table[chan], index2, axis=1, mode="promise_in_bounds")
                value.append(base + frac * diff)
            extinction = value[3] * (1.25 - 1.0 / (1.0 + slope))
            passed = transmit * jnp.exp(-step * extinction)
            weight = transmit - passed
            for chan in range(3):
                colors[chan] = colors[chan] + weight * value[chan]
            transmit = passed
            below, here = here, above
        for chan in range(3):
            out_ref[i, chan] = colors[chan]
        out_ref[i, 3] = transmit
        return carry

    lax.fori_loop(0, rows // SUB, block, 0)


def combine_kernel(slab_ref, out_ref):
    count = slab_ref.shape[0]
    transmit = slab_ref[0, 3]
    colors = [slab_ref[0, chan] for chan in range(3)]
    for k in range(1, count):
        for chan in range(3):
            colors[chan] = colors[chan] + transmit * slab_ref[k, chan]
        transmit = transmit * slab_ref[k, 3]
    for chan in range(3):
        out_ref[chan] = colors[chan]
    out_ref[3] = 1.0 - transmit


def on_device(qtensor, labels, tables):
    _, nz, rows, lanes = qtensor.shape
    groups = lax.axis_size("depth")
    across = lax.axis_size("cols")
    step = 2.0 / (nz * groups)
    params = pltpu.CompilerParams(vmem_limit_bytes=32 * 1024 * 1024)
    f32 = lambda *shape: jax.ShapeDtypeStruct(shape, jnp.float32)
    layer = f32(rows, lanes)
    column = f32(nz, rows)
    s, first, last, colfirst, collast = pl.pallas_call(
        strength_kernel,
        out_shape=[f32(nz, rows + 2 * PAD, lanes), layer, layer, column, column],
        scratch_shapes=[pltpu.VMEM((rows, lanes), jnp.float32), pltpu.VMEM((lanes, rows), jnp.float32)],
        compiler_params=params,
        name="strength",
    )(qtensor)

    up = lambda n: [(i, (i + 1) % n) for i in range(n)]
    down = lambda n: [(i, (i - 1) % n) for i in range(n)]
    left = lax.ppermute(collast, "cols", up(across))
    right = lax.ppermute(colfirst, "cols", down(across))
    before = lax.ppermute(last, "depth", up(groups))
    after = lax.ppermute(first, "depth", down(groups))

    slabs = pl.pallas_call(
        functools.partial(shade_kernel, step),
        out_shape=f32(rows // SUB, 4, SUB, lanes),
        scratch_shapes=[
            pltpu.VMEM((tables.shape[0], SUB, lanes), jnp.float32),
            pltpu.VMEM((lanes, rows), jnp.float32),
            pltpu.VMEM((rows, lanes), jnp.float32),
        ],
        compiler_params=params,
        name="shade",
    )(tables, s, labels, before, after, left, right)

    mine = lax.all_to_all(slabs, "depth", 0, 0)
    return pl.pallas_call(
        combine_kernel, out_shape=f32(4, SUB, lanes), compiler_params=params, name="combine"
    )(mine)


def solution(mesh):
    placed = (P(None, "depth", None, "cols"), P("depth", None, "cols"), P())
    return jax.shard_map(
        on_device, mesh=mesh, in_specs=placed, out_specs=P(None, "depth", "cols"), check_vma=False
    )
```

time: 233 us -> 30.5 us (0.13)
  the two profiles are of different devices: /device:TPU:38 before, /device:TPU:0 now
where the time goes in v1:
time: 30.5 us; the launch traced here: 30.3 us
  blocking collectives  12.9 us (42%)
  starting transfers between devices  8.64 us (28%)
  Pallas kernels  6.11 us (20%)
  waiting for transfers between devices  1.33 us (4%)
  local copies, waits for them, and re-layouts  1.32 us (4%)
    all_to_all x1, blocking collectives, on_device(): mine = lax.all_to_all(slabs, 'depth', 0, 0)  12.9 us
    pallas_call x1, Pallas kernels, on_device(): pl.pallas_call(functools.partial(shade_kernel, step), out_shape=f32(rows...  4.61 us
    ppermute x1, starting transfers between devices, on_device(): after = lax.ppermute(first, 'depth', down(groups))  3.71 us
    ppermute x1, starting transfers between devices, on_device(): right = lax.ppermute(colfirst, 'cols', down(across))  3.2 us
    ppermute x1, starting transfers between devices, on_device(): before = lax.ppermute(last, 'depth', up(groups))  1.73 us
    unnamed x6, local copies, waits for them, and re-layouts  1.32 us
    ppermute x1, waiting for transfers between devices, on_device(): left = lax.ppermute(collast, 'cols', up(across))  1.29 us
    pallas_call x1, Pallas kernels, on_device(): pl.pallas_call(strength_kernel, out_shape=[f32(nz, rows + 2 * PAD, lanes)...  0.87 us
  transfers between devices with their start and end apart: 4, of which 1 were waited for; matrix products, arithmetic and copies ran while one was open for 0% of the time, Pallas kernels for 0%

profile of v1, /device:TPU:0, one launch (start us, length us, event | category | flops | bytes accessed | tf_op | source)
XLA Modules:
  0.0 30.3 jit_solution(11288654537748207800)
XLA Ops:
  0.0 0.0 copy-start
  0.0 1.3 %copy-done = bf16[5,8,128,128]{3,2,1,0:T(8,128)(2,1)S(1)} copy-done((bf16[5,8,128,128]{3,2,1,0:T(8,128)(2,1)S(1)}, bf16[5,8,128,128]{3,2,1,0:T(8,128)(2,1)}, u32[]{:S(2)}) %copy-start) | copy-done | bytes 1310744
  1.3 0.0 copy-start.1
  1.3 0.0 copy-start.2
  1.3 0.9 %strength.1 = (f32[8,144,128]{2,1,0:T(8,128)S(1)}, f32[128,128]{1,0:T(8,128)S(1)}, f32[128,128]{1,0:T(8,128)S(1)}, f32[8,128]{1,0:T(8,128)S(1)}, f32[8,128]{1,0:T(8,128)S(1)}) custom-call(bf16[5,8,128,128]{3,2,1,0:T(8,128)(2,1)S(1)} %copy-done), custom_call_target="tpu_custom_call" | custom-call | tf_op jit(solution)/shard_map/strength/pallas_call | solution.py:138
  2.2 1.7 %collective-permute-start = (f32[128,128]{1,0:T(8,128)S(1)}, f32[128,128]{1,0:T(8,128)S(1)}, u32[]{:S(2)}, u32[]{:S(2)}) collective-permute-start(f32[128,128]{1,0:T(8,128)S(1)} %get-tuple-element.11), channel_id=1, source_target_pairs={{0,1},{1,2},{2,3},{3,4},{4,5},{5,6},{6,7},{7,8},{8,9},{9,10},{10,1... | collective-permute-start | bytes 196616 | tf_op jit(solution)/shard_map/ppermute | solution.py:150
  3.9 3.7 %collective-permute-start.1 = (f32[128,128]{1,0:T(8,128)S(1)}, f32[128,128]{1,0:T(8,128)S(1)}, u32[]{:S(2)}, u32[]{:S(2)}) collective-permute-start(f32[128,128]{1,0:T(8,128)S(1)} %get-tuple-element.12), channel_id=1, source_target_pairs={{0,15},{1,0},{2,1},{3,2},{4,3},{5,4},{6,5},{7,6},{8,7},{9,8},{10,9... | collective-permute-start | bytes 196616 | tf_op jit(solution)/shard_map/ppermute | solution.py:151
  7.6 0.0 collective-permute-start.2
  7.6 3.2 %collective-permute-start.3 = (f32[8,128]{1,0:T(8,128)S(1)}, f32[8,128]{1,0:T(8,128)S(1)}, u32[]{:S(2)}, u32[]{:S(2)}) collective-permute-start(f32[8,128]{1,0:T(8,128)S(1)} %get-tuple-element.14), channel_id=1, source_target_pairs={{0,112},{16,0},{32,16},{48,32},{64,48},{80,64},{96,80},{112,96},{1... | collective-permute-start | bytes 12296 | tf_op jit(solution)/shard_map/ppermute | solution.py:149
  10.8 1.3 %collective-permute-done.2.left_ref = f32[8,128]{1,0:T(8,128)S(1)} collective-permute-done((f32[8,128]{1,0:T(8,128)S(1)}, f32[8,128]{1,0:T(8,128)S(1)}, u32[]{:S(2)}, u32[]{:S(2)}) %collective-permute-start.2) | collective-permute-done | bytes 4128 | tf_op jit(solution)/shard_map/ppermute | solution.py:148
  12.1 0.0 collective-permute-done.3.right_ref
  12.2 0.0 collective-permute-done.before_ref
  12.2 0.0 collective-permute-done.1.after_ref
  12.2 0.0 copy-done.1
  12.2 0.0 copy-done.2
  12.2 4.6 %shade.1 = f32[16,4,8,128]{3,2,1,0:T(8,128)S(1)} custom-call(f32[4,4,16]{2,1,0:T(4,128)S(1)} %copy-done.2, f32[8,144,128]{2,1,0:T(8,128)S(1)} %get-tuple-element.10.s_ref, s32[8,128,128]{2,1,0:T(8,128)S(1)} %copy-done.1, f32[128,128]{1,0:T(8,128)S(1)} %collective-permute-done.before_ref, f32[128,128]{1,0:T(8,128)S(1)} %collective-permute-done.1.after_ref, ...), custom_call_target="tpu_custom_call" | custom-call | tf_op jit(solution)/shard_map/shade/pallas_call | solution.py:153
  16.8 12.9 %all_to_all.5.slab_ref = f32[16,4,8,128]{3,2,1,0:T(8,128)S(1)} all-to-all(f32[16,4,8,128]{3,2,1,0:T(8,128)S(1)} %shade.1), channel_id=1, replica_groups=mesh['cols'=8,'depth'=16] {'depth'}, dimensions={0} | all-to-all | bytes 524288 | tf_op jit(solution)/shard_map/all_to_all | solution.py:165
  29.7 0.6 %combine.1 = f32[4,8,128]{2,1,0:T(8,128)} custom-call(f32[16,4,8,128]{3,2,1,0:T(8,128)S(1)} %all_to_all.5.slab_ref), custom_call_target="tpu_custom_call" | custom-call | tf_op jit(solution)/shard_map/combine/pallas_call | solution.py:166
Async XLA Ops:
  0.0 1.3 %copy-start = (bf16[5,8,128,128]{3,2,1,0:T(8,128)(2,1)S(1)}, bf16[5,8,128,128]{3,2,1,0:T(8,128)(2,1)}, u32[]{:S(2)}) copy-start(bf16[5,8,128,128]{3,2,1,0:T(8,128)(2,1)} %q_ref.1) | copy-start | bytes 3932164
  1.3 10.9 %copy-start.1 = (s32[8,128,128]{2,1,0:T(8,128)S(1)}, s32[8,128,128]{2,1,0:T(8,128)}, u32[]{:S(2)}) copy-start(s32[8,128,128]{2,1,0:T(8,128)} %lab_ref.1) | copy-start | bytes 1572868
  1.3 10.9 %copy-start.2 = (f32[4,4,16]{2,1,0:T(4,128)S(1)}, f32[4,4,16]{2,1,0:T(4,128)}, u32[]{:S(2)}) copy-start(f32[4,4,16]{2,1,0:T(4,128)} %tab_ref.1) | copy-start | bytes 3076
  2.2 10.0 %collective-permute-start = (f32[128,128]{1,0:T(8,128)S(1)}, f32[128,128]{1,0:T(8,128)S(1)}, u32[]{:S(2)}, u32[]{:S(2)}) collective-permute-start(f32[128,128]{1,0:T(8,128)S(1)} %get-tuple-element.11), channel_id=1, source_target_pairs={{0,1},{1,2},{2,3},{3,4},{4,5},{5,6},{6,7},{7,8},{8,9},{9,10},{10,1... | collective-permute-start | bytes 196616 | tf_op jit(solution)/shard_map/ppermute | solution.py:150
  3.9 8.2 %collective-permute-start.1 = (f32[128,128]{1,0:T(8,128)S(1)}, f32[128,128]{1,0:T(8,128)S(1)}, u32[]{:S(2)}, u32[]{:S(2)}) collective-permute-start(f32[128,128]{1,0:T(8,128)S(1)} %get-tuple-element.12), channel_id=1, source_target_pairs={{0,15},{1,0},{2,1},{3,2},{4,3},{5,4},{6,5},{7,6},{8,7},{9,8},{10,9... | collective-permute-start | bytes 196616 | tf_op jit(solution)/shard_map/ppermute | solution.py:151
  7.6 4.5 %collective-permute-start.2 = (f32[8,128]{1,0:T(8,128)S(1)}, f32[8,128]{1,0:T(8,128)S(1)}, u32[]{:S(2)}, u32[]{:S(2)}) collective-permute-start(f32[8,128]{1,0:T(8,128)S(1)} %get-tuple-element.13), channel_id=1, source_target_pairs={{0,16},{16,32},{32,48},{48,64},{64,80},{80,96},{96,112},{112,0},{1... | collective-permute-start | bytes 12296 | tf_op jit(solution)/shard_map/ppermute | solution.py:148
  7.6 4.5 %collective-permute-start.3 = (f32[8,128]{1,0:T(8,128)S(1)}, f32[8,128]{1,0:T(8,128)S(1)}, u32[]{:S(2)}, u32[]{:S(2)}) collective-permute-start(f32[8,128]{1,0:T(8,128)S(1)} %get-tuple-element.14), channel_id=1, source_target_pairs={{0,112},{16,0},{32,16},{48,32},{64,48},{80,64},{96,80},{112,96},{1... | collective-permute-start | bytes 12296 | tf_op jit(solution)/shard_map/ppermute | solution.py:149

commit v2 on v1

v2 whole, which is shorter than its diff:
```python
import functools
import jax
import jax.numpy as jnp
from jax import lax
from jax.experimental import pallas as pl
from jax.experimental.pallas import tpu as pltpu
from jax.sharding import PartitionSpec as P

SUB = 8
PAD = 8
CHUNKS = 1
BLOCK = 128


def strength_kernel(q_ref, lab_ref, tab_ref, s_ref, first_ref, last_ref, colfirst_ref, collast_ref, lab_here, knots_ref, q_here, sems, tab_here, rows_tab, edge, edge_t):
    _, nz, rows, lanes = q_here.shape
    part = nz // CHUNKS
    copies = []
    for k in range(CHUNKS):
        at = pl.ds(k * part, part)
        copies.append(pltpu.make_async_copy(q_ref.at[:, at], q_here.at[:, at], sems.at[k]))
        copies[k].start()
    tab_copy = pltpu.make_async_copy(tab_ref, tab_here, sems.at[CHUNKS])
    tab_copy.start()
    lab_copy = pltpu.make_async_copy(lab_ref, lab_here, sems.at[CHUNKS + 1])
    lab_copy.start()
    lane = lax.broadcasted_iota(jnp.int32, (BLOCK, lanes), 1)
    zeros = jnp.zeros((PAD, lanes), jnp.float32)
    for z in range(nz):
        s_ref[z, 0:PAD, :] = zeros
        s_ref[z, PAD + rows:, :] = zeros

    nlab, nchan, nbins = tab_here.shape
    rows_tab[...] = jnp.zeros_like(rows_tab)
    tab_copy.wait()
    for lab in range(nlab):
        rows_tab[lab, 0:nchan, 0:nbins] = tab_here[lab]
    knots = rows_tab[0]
    for lab in range(1, nlab):
        knots = knots + pltpu.roll(rows_tab[lab], lab * nbins, 1)
    knots_ref[0] = knots
    knots_ref[1] = pltpu.roll(knots, lanes - 1, 1) - knots

    for k in range(CHUNKS):
        copies[k].wait()

        def block(i, carry, k=k):
            r0 = pl.multiple_of(i * BLOCK, BLOCK)
            packed = edge[pl.ds(r0, BLOCK), :]
            for z in range(k * part, (k + 1) * part):
                q = [q_here[c, z, pl.ds(r0, BLOCK), :].astype(jnp.float32) for c in range(5)]
                s = 3.0 * (q[0] * q[0] + q[3] * q[3] + q[0] * q[3] + q[1] * q[1] + q[2] * q[2] + q[4] * q[4])
                s_ref[z, pl.ds(r0 + PAD, BLOCK), :] = s
                if z == 0:
                    first_ref[pl.ds(r0, BLOCK), :] = s
                if z == nz - 1:
                    last_ref[pl.ds(r0, BLOCK), :] = s
                turned = pltpu.roll(s, 2 * z + 1, 1)
                packed = jnp.where(lane >> 1 == z, turned, packed)
            edge[pl.ds(r0, BLOCK), :] = packed
            return carry

        lax.fori_loop(0, rows // BLOCK, block, 0)
    edge_t[...] = edge[...].T
    collast_ref[...] = edge_t[pl.ds(0, nz, stride=2), :]
    colfirst_ref[...] = edge_t[pl.ds(1, nz, stride=2), :]
    lab_copy.wait()


def lookup_kernel(nbins, knots_ref, s_ref, lab_ref, value_ref, part_ref, edge_ref):
    nz, rows, lanes = lab_ref.shape
    nchan = value_ref.shape[0]
    lane = lax.broadcasted_iota(jnp.int32, (SUB, lanes), 1)
    inner = (lane > 0) & (lane < lanes - 1)
    base = [jnp.broadcast_to(knots_ref[0, k:k + 1, :], (SUB, lanes)) for k in range(nchan)]
    diff = [jnp.broadcast_to(knots_ref[1, k:k + 1, :], (SUB, lanes)) for k in range(nchan)]

    def block(i, carry):
        r0 = pl.multiple_of(i * SUB, SUB)
        at = pl.ds(r0, SUB)
        packed = jnp.zeros((SUB, lanes), jnp.float32)
        below = None
        here = s_ref[0, pl.ds(r0 + PAD, SUB), :]
        for z in range(nz):
            above = s_ref[z + 1, pl.ds(r0 + PAD, SUB), :] if z < nz - 1 else None
            dx = pltpu.roll(here, lanes - 1, 1) - pltpu.roll(here, 1, 1)
            packed = jnp.where(lane >> 1 == z, pltpu.roll(dx, 2 * z + 1, 1), packed)
            dy = s_ref[z, pl.ds(r0 + PAD + 1, SUB), :] - s_ref[z, pl.ds(r0 + PAD - 1, SUB), :]
            part = dy * dy + jnp.where(inner, dx * dx, 0.0)
            if 0 < z < nz - 1:
                dz = above - below
                part = part + dz * dz
            part_ref[z, at, :] = part
            coord = jnp.clip(2.0 * here, 0.0, nbins - 1.0)
            knot = coord.astype(jnp.int32)
            frac = coord - knot.astype(jnp.float32)
            index = lab_ref[z, at, :] * nbins + knot
            for chan in range(nchan):
                low = jnp.take_along_axis(base[chan], index, axis=1, mode="promise_in_bounds")
                rise = jnp.take_along_axis(diff[chan], index, axis=1, mode="promise_in_bounds")
                value_ref[chan, z, at, :] = low + frac * rise
            below, here = here, above
        edge_ref[at, :] = packed
        return carry

    lax.fori_loop(0, rows // SUB, block, 0)


def finish_kernel(step, value_ref, part_ref, edge_ref, s_ref, colfirst_ref, collast_ref, before_ref, after_ref, left_ref, right_ref,
                  out_ref, halo, halo_t):
    _, nz, rows, lanes = value_ref.shape
    d = lax.axis_index("depth")
    c = lax.axis_index("cols")
    has_before = (d > 0).astype(jnp.float32)
    has_after = (d < lax.axis_size("depth") - 1).astype(jnp.float32)
    has_left = (c > 0).astype(jnp.float32)
    has_right = (c < lax.axis_size("cols") - 1).astype(jnp.float32)
    lane = lax.broadcasted_iota(jnp.int32, (SUB, lanes), 1)
    outer = (lane == 0) | (lane == lanes - 1)

    halo[pl.ds(0, nz, stride=2), :] = right_ref[...] * has_right - colfirst_ref[...]
    halo[pl.ds(1, nz, stride=2), :] = collast_ref[...] - left_ref[...] * has_left
    halo_t[...] = halo[...].T

    def block(i, carry):
        r0 = pl.multiple_of(i * SUB, SUB)
        at = pl.ds(r0, SUB)
        inside = pl.ds(r0 + PAD, SUB)
        sides = halo_t[at, :] + edge_ref[at, :]
        sides = sides * sides
        transmit = jnp.ones((SUB, lanes), jnp.float32)
        colors = [jnp.zeros((SUB, lanes), jnp.float32) for _ in range(3)]
        for z in range(nz):
            slope4 = part_ref[z, at, :] + jnp.where(outer, pltpu.roll(sides, lanes - 1 - 2 * z, 1), 0.0)
            if z == 0:
                dz = s_ref[1, inside, :] - before_ref[at, :] * has_before
                slope4 = slope4 + dz * dz
            if z == nz - 1:
                dz = after_ref[at, :] * has_after - s_ref[nz - 2, inside, :]
                slope4 = slope4 + dz * dz
            extinction = value_ref[3, z, at, :] * (1.25 - 4.0 / (4.0 + slope4))
            passed = transmit * jnp.exp(-step * extinction)
            weight = transmit - passed
            for chan in range(3):
                colors[chan] = colors[chan] + weight * value_ref[chan, z, at, :]
            transmit = passed
        for chan in range(3):
            out_ref[i, chan] = colors[chan]
        out_ref[i, 3] = transmit
        return carry

    lax.fori_loop(0, rows // SUB, block, 0, unroll=2)


def combine_kernel(slab_ref, out_ref):
    count = slab_ref.shape[0]
    transmit = slab_ref[0, 3]
    colors = [slab_ref[0, chan] for chan in range(3)]
    for k in range(1, count):
        for chan in range(3):
            colors[chan] = colors[chan] + transmit * slab_ref[k, chan]
        transmit = transmit * slab_ref[k, 3]
    for chan in range(3):
        out_ref[chan] = colors[chan]
    out_ref[3] = 1.0 - transmit


def on_device(qtensor, labels, tables):
    _, nz, rows, lanes = qtensor.shape
    groups = lax.axis_size("depth")
    across = lax.axis_size("cols")
    step = 2.0 / (nz * groups)
    params = pltpu.CompilerParams(vmem_limit_bytes=32 * 1024 * 1024)
    f32 = lambda *shape: jax.ShapeDtypeStruct(shape, jnp.float32)
    layer = f32(rows, lanes)
    column = f32(nz, rows)
    plane = pltpu.VMEM((rows, lanes), jnp.float32)
    nlab, nchan, nbins = tables.shape
    far = lambda array: pltpu.with_memory_space_constraint(array, pltpu.HBM)
    s, first, last, colfirst, collast, labels, knots = pl.pallas_call(
        strength_kernel,
        in_specs=[pl.BlockSpec(memory_space=pltpu.HBM)] * 3,
        out_shape=[
            f32(nz, rows + 2 * PAD, lanes), layer, layer, column, column,
            jax.ShapeDtypeStruct(labels.shape, labels.dtype), f32(2, SUB, lanes),
        ],
        scratch_shapes=[
            pltpu.VMEM(qtensor.shape, qtensor.dtype),
            pltpu.SemaphoreType.DMA((CHUNKS + 2,)),
            pltpu.VMEM(tables.shape, jnp.float32),
            pltpu.VMEM((nlab, SUB, lanes), jnp.float32),
            plane,
            pltpu.VMEM((lanes, rows), jnp.float32),
        ],
        compiler_params=params,
        name="strength",
    )(far(qtensor), far(labels), far(tables))

    up = lambda n: [(i, (i + 1) % n) for i in range(n)]
    down = lambda n: [(i, (i - 1) % n) for i in range(n)]
    left = lax.ppermute(collast, "cols", up(across))
    right = lax.ppermute(colfirst, "cols", down(across))
    before = lax.ppermute(last, "depth", up(groups))
    after = lax.ppermute(first, "depth", down(groups))

    value, part, edge = pl.pallas_call(
        functools.partial(lookup_kernel, nbins),
        out_shape=[f32(nchan, nz, rows, lanes), f32(nz, rows, lanes), layer],
        compiler_params=params,
        cost_estimate=pl.CostEstimate(flops=60 * nz * rows * lanes, bytes_accessed=28 * nz * rows * lanes, transcendentals=0),
        name="lookup",
    )(knots, s, labels)

    slabs = pl.pallas_call(
        functools.partial(finish_kernel, step),
        out_shape=f32(rows // SUB, 4, SUB, lanes),
        scratch_shapes=[pltpu.VMEM((lanes, rows), jnp.float32), plane],
        compiler_params=params,
        name="finish",
    )(value, part, edge, s, colfirst, collast, before, after, left, right)

    mine = lax.all_to_all(slabs, "depth", 0, 0)
    return pl.pallas_call(
        combine_kernel, out_shape=f32(4, SUB, lanes), compiler_params=params, name="combine"
    )(mine)


def solution(mesh):
    placed = (P(None, "depth", None, "cols"), P("depth", None, "cols"), P())
    return jax.shard_map(
        on_device, mesh=mesh, in_specs=placed, out_specs=P(None, "depth", "cols"), check_vma=False
    )
```

time: 30.5 us -> 27.9 us (0.915)
  local copies, waits for them, and re-layouts: 1.32 us -> 0 us
  waiting for transfers between devices: 1.33 us -> 0.01 us
  Pallas kernels: 6.11 us -> 7.26 us
  blocking collectives: 12.9 us -> 11.8 us
    unnamed x6 -> x0, local copies, waits for them, and re-layouts: 1.32 us -> none
    ppermute x1, waiting for transfers between devices: 1.29 us -> 0.01 us  [on_device(): left = lax.ppermute(collast, 'cols', up(across))]
    pallas_call x2 -> x3, Pallas kernels: 5.48 us -> 6.63 us  [the longest x1 3.82 us: on_device(): pl.pallas_call(functools.partial(lookup_kernel, nbins), out_shape=[f32(nc...]
    all_to_all x1, blocking collectives: 12.9 us -> 11.8 us  [on_device(): mine = lax.all_to_all(slabs, 'depth', 0, 0)]
  transfers between devices with their start and end apart: 4 -> 4, of which waited for: 1 -> 0; matrix products, arithmetic and copies ran while one was open for 0% -> 0% of each run, Pallas kernels for 0% -> 14%
where the time goes in v2:
time: 27.9 us; the launch traced here: 27.8 us
  blocking collectives  11.8 us (42%)
  starting transfers between devices  8.64 us (31%)
  Pallas kernels  7.26 us (26%)
    all_to_all x1, blocking collectives, on_device(): mine = lax.all_to_all(slabs, 'depth', 0, 0)  11.8 us
    pallas_call x1, Pallas kernels, on_device(): pl.pallas_call(functools.partial(lookup_kernel, nbins), out_shape=[f32(nc...  3.82 us
    ppermute x1, starting transfers between devices, on_device(): after = lax.ppermute(first, 'depth', down(groups))  3.71 us
    ppermute x1, starting transfers between devices, on_device(): right = lax.ppermute(colfirst, 'cols', down(across))  3.2 us
    ppermute x1, starting transfers between devices, on_device(): before = lax.ppermute(last, 'depth', up(groups))  1.73 us
    pallas_call x1, Pallas kernels, on_device(): pl.pallas_call(strength_kernel, in_specs=[pl.BlockSpec(memory_space=pltpu...  1.72 us
    pallas_call x1, Pallas kernels, on_device(): pl.pallas_call(functools.partial(finish_kernel, step), out_shape=f32(rows...  1.09 us
    pallas_call x1, Pallas kernels, on_device(): pl.pallas_call(combine_kernel, out_shape=f32(4, SUB, lanes), compiler_par...  0.63 us
  transfers between devices with their start and end apart: 4, of which 0 were waited for; matrix products, arithmetic and copies ran while one was open for 0% of the time, Pallas kernels for 14%

profile of v2, /device:TPU:0, one launch (start us, length us, event | category | flops | bytes accessed | tf_op | source)
XLA Modules:
  0.0 27.8 jit_solution(13688116252285259678)
XLA Ops:
  0.0 1.7 %strength.1 = (f32[8,144,128]{2,1,0:T(8,128)S(1)}, f32[128,128]{1,0:T(8,128)S(1)}, f32[128,128]{1,0:T(8,128)S(1)}, f32[8,128]{1,0:T(8,128)S(1)}, f32[8,128]{1,0:...) custom-call(bf16[5,8,128,128]{3,2,1,0:T(8,128)(2,1)} %q_ref.1, s32[8,128,128]{2,1,0:T(8,128)} %lab_ref.1, ...), custom_call_target="tpu_custom_call" | custom-call | tf_op jit(solution)/shard_map/strength/pallas_call | solution.py:180
  1.7 1.7 %collective-permute-start = (f32[128,128]{1,0:T(8,128)S(1)}, f32[128,128]{1,0:T(8,128)S(1)}, u32[]{:S(2)}, u32[]{:S(2)}) collective-permute-start(f32[128,128]{1,0:T(8,128)S(1)} %get-tuple-element.23), channel_id=1, source_target_pairs={{0,1},{1,2},{2,3},{3,4},{4,5},{5,6},{6,7},{7,8},{8,9},{9,10},{10,1... | collective-permute-start | bytes 196616 | tf_op jit(solution)/shard_map/ppermute | solution.py:203
  3.5 3.7 %collective-permute-start.1 = (f32[128,128]{1,0:T(8,128)S(1)}, f32[128,128]{1,0:T(8,128)S(1)}, u32[]{:S(2)}, u32[]{:S(2)}) collective-permute-start(f32[128,128]{1,0:T(8,128)S(1)} %get-tuple-element.24), channel_id=1, source_target_pairs={{0,15},{1,0},{2,1},{3,2},{4,3},{5,4},{6,5},{7,6},{8,7},{9,8},{10,9... | collective-permute-start | bytes 196616 | tf_op jit(solution)/shard_map/ppermute | solution.py:204
  7.2 0.0 collective-permute-start.2
  7.2 3.2 %collective-permute-start.3 = (f32[8,128]{1,0:T(8,128)S(1)}, f32[8,128]{1,0:T(8,128)S(1)}, u32[]{:S(2)}, u32[]{:S(2)}) collective-permute-start(f32[8,128]{1,0:T(8,128)S(1)} %get-tuple-element.21.colfirst_ref), channel_id=1, source_target_pairs={{0,112},{16,0},{32,16},{48,32},{64,48},{80,64},{96,80},{112,96},{1... | collective-permute-start | bytes 12296 | tf_op jit(solution)/shard_map/ppermute | solution.py:202
  10.4 3.8 %lookup.1 = (f32[4,8,128,128]{3,2,1,0:T(8,128)S(1)}, f32[8,128,128]{2,1,0:T(8,128)S(1)}, f32[128,128]{1,0:T(8,128)S(1)}) custom-call(f32[2,8,128]{2,1,0:T(8,128)S(1)} %get-tuple-element.15.knots_ref, f32[8,144,128]{2,1,0:T(8,128)S(1)} %get-tuple-element.16.s_ref, s32[8,128,128]{2,1,0:T(8,128)S(1)} %get-tuple-element.17.lab_ref), custom_call_target="tpu_custom_call" | custom-call | flops 7864320 | bytes 3670016 | tf_op jit(solution)/shard_map/lookup/pallas_call | solution.py:206
  14.2 0.0 collective-permute-done.2.left_ref
  14.2 0.0 collective-permute-done.3.right_ref
  14.2 0.0 collective-permute-done.before_ref
  14.2 0.0 collective-permute-done.1.after_ref
  14.2 1.1 %finish.1 = f32[16,4,8,128]{3,2,1,0:T(8,128)S(1)} custom-call(f32[4,8,128,128]{3,2,1,0:T(8,128)S(1)} %get-tuple-element.18.value_ref, f32[8,128,128]{2,1,0:T(8,128)S(1)} %get-tuple-element.19.part_ref, f32[128,128]{1,0:T(8,128)S(1)} %get-tuple-element.20.edge_ref, f32[8,144,128]{2,1,0:T(8,128)S(1)} %get-tuple-element.16.s_ref, ...), custom_call_target="tpu_custom_call" | custom-call | tf_op jit(solution)/shard_map/finish/pallas_call | solution.py:214
  15.3 11.8 %all_to_all.5.slab_ref = f32[16,4,8,128]{3,2,1,0:T(8,128)S(1)} all-to-all(f32[16,4,8,128]{3,2,1,0:T(8,128)S(1)} %finish.1), channel_id=1, replica_groups=mesh['cols'=8,'depth'=16] {'depth'}, dimensions={0} | all-to-all | bytes 524288 | tf_op jit(solution)/shard_map/all_to_all | solution.py:222
  27.1 0.6 %combine.1 = f32[4,8,128]{2,1,0:T(8,128)} custom-call(f32[16,4,8,128]{3,2,1,0:T(8,128)S(1)} %all_to_all.5.slab_ref), custom_call_target="tpu_custom_call" | custom-call | tf_op jit(solution)/shard_map/combine/pallas_call | solution.py:223
Async XLA Ops:
  1.7 12.5 %collective-permute-start = (f32[128,128]{1,0:T(8,128)S(1)}, f32[128,128]{1,0:T(8,128)S(1)}, u32[]{:S(2)}, u32[]{:S(2)}) collective-permute-start(f32[128,128]{1,0:T(8,128)S(1)} %get-tuple-element.23), channel_id=1, source_target_pairs={{0,1},{1,2},{2,3},{3,4},{4,5},{5,6},{6,7},{7,8},{8,9},{9,10},{10,1... | collective-permute-start | bytes 196616 | tf_op jit(solution)/shard_map/ppermute | solution.py:203
  3.5 10.8 %collective-permute-start.1 = (f32[128,128]{1,0:T(8,128)S(1)}, f32[128,128]{1,0:T(8,128)S(1)}, u32[]{:S(2)}, u32[]{:S(2)}) collective-permute-start(f32[128,128]{1,0:T(8,128)S(1)} %get-tuple-element.24), channel_id=1, source_target_pairs={{0,15},{1,0},{2,1},{3,2},{4,3},{5,4},{6,5},{7,6},{8,7},{9,8},{10,9... | collective-permute-start | bytes 196616 | tf_op jit(solution)/shard_map/ppermute | solution.py:204
  7.2 7.0 %collective-permute-start.2 = (f32[8,128]{1,0:T(8,128)S(1)}, f32[8,128]{1,0:T(8,128)S(1)}, u32[]{:S(2)}, u32[]{:S(2)}) collective-permute-start(f32[8,128]{1,0:T(8,128)S(1)} %get-tuple-element.22.collast_ref), channel_id=1, source_target_pairs={{0,16},{16,32},{32,48},{48,64},{64,80},{80,96},{96,112},{112,0},{1... | collective-permute-start | bytes 12296 | tf_op jit(solution)/shard_map/ppermute | solution.py:201
  7.2 7.0 %collective-permute-start.3 = (f32[8,128]{1,0:T(8,128)S(1)}, f32[8,128]{1,0:T(8,128)S(1)}, u32[]{:S(2)}, u32[]{:S(2)}) collective-permute-start(f32[8,128]{1,0:T(8,128)S(1)} %get-tuple-element.21.colfirst_ref), channel_id=1, source_target_pairs={{0,112},{16,0},{32,16},{48,32},{64,48},{80,64},{96,80},{112,96},{1... | collective-permute-start | bytes 12296 | tf_op jit(solution)/shard_map/ppermute | solution.py:202

commit v3 on v2

--- a/solution.py
+++ b/solution.py
@@ -106,7 +106,7 @@
     lax.fori_loop(0, rows // SUB, block, 0)
 
 
-def finish_kernel(step, value_ref, part_ref, edge_ref, s_ref, colfirst_ref, collast_ref, before_ref, after_ref, left_ref, right_ref,
+def finish_kernel(step, value_ref, part_ref, edge_ref, s_ref, colfirst_ref, collast_ref, before_ref, swap1_ref, swap0_ref, after_ref,
                   out_ref, halo, halo_t):
     _, nz, rows, lanes = value_ref.shape
     d = lax.axis_index("depth")
@@ -118,8 +118,11 @@
     lane = lax.broadcasted_iota(jnp.int32, (SUB, lanes), 1)
     outer = (lane == 0) | (lane == lanes - 1)
 
-    halo[pl.ds(0, nz, stride=2), :] = right_ref[...] * has_right - colfirst_ref[...]
-    halo[pl.ds(1, nz, stride=2), :] = collast_ref[...] - left_ref[...] * has_left
+    odd = c % 2 == 1
+    left = jnp.where(odd, swap0_ref[...], swap1_ref[...])
+    right = jnp.where(odd, swap1_ref[...], swap0_ref[...])
+    halo[pl.ds(0, nz, stride=2), :] = right * has_right - colfirst_ref[...]
+    halo[pl.ds(1, nz, stride=2), :] = collast_ref[...] - left * has_left
     halo_t[...] = halo[...].T
 
     def block(i, carry):
@@ -198,10 +201,17 @@
 
     up = lambda n: [(i, (i + 1) % n) for i in range(n)]
     down = lambda n: [(i, (i - 1) % n) for i in range(n)]
-    left = lax.ppermute(collast, "cols", up(across))
-    right = lax.ppermute(colfirst, "cols", down(across))
+    after = lax.ppermute(first, "depth", down(groups))
     before = lax.ppermute(last, "depth", up(groups))
-    after = lax.ppermute(first, "depth", down(groups))
+    c_odd = lax.axis_index("cols") % 2 == 1
+    inner = [(i, i ^ 1) for i in range(across)]
+    outer = []
+    for i in range(across):
+        j = ((i + 1) ^ 1) - 1
+        for g in range(groups):
+            outer.append((i * groups + g, j * groups + g if 0 <= j < across else i * groups + (g ^ 1)))
+    swap0 = lax.ppermute(jnp.where(c_odd, colfirst, collast), "cols", inner)
+    swap1 = lax.ppermute(jnp.where(c_odd, collast, colfirst), ("cols", "depth"), outer)
 
     value, part, edge = pl.pallas_call(
         functools.partial(lookup_kernel, nbins),
@@ -217,7 +227,7 @@
         scratch_shapes=[pltpu.VMEM((lanes, rows), jnp.float32), plane],
         compiler_params=params,
         name="finish",
-    )(value, part, edge, s, colfirst, collast, before, after, left, right)
+    )(value, part, edge, s, colfirst, collast, before, swap1, swap0, after)
 
     mine = lax.all_to_all(slabs, "depth", 0, 0)
     return pl.pallas_call(

time: 27.9 us -> 27.2 us (0.975)
  starting transfers between devices: 8.64 us -> 7.53 us
  blocking collectives: 11.8 us -> 12.2 us
    ppermute x2, starting transfers between devices: 3.2 us -> 2.09 us  [the longest x1 2.09 us: on_device(): swap0 = lax.ppermute(jnp.where(c_odd, colfirst, collast), 'cols', inner)]
    all_to_all x1, blocking collectives: 11.8 us -> 12.2 us  [on_device(): mine = lax.all_to_all(slabs, 'depth', 0, 0)]
where the time goes in v3:
time: 27.2 us; the launch traced here: 27.1 us
  blocking collectives  12.2 us (45%)
  starting transfers between devices  7.53 us (28%)
  Pallas kernels  7.27 us (27%)
    all_to_all x1, blocking collectives, on_device(): mine = lax.all_to_all(slabs, 'depth', 0, 0)  12.2 us
    pallas_call x1, Pallas kernels, on_device(): pl.pallas_call(functools.partial(lookup_kernel, nbins), out_shape=[f32(nc...  3.82 us
    ppermute x1, starting transfers between devices, on_device(): after = lax.ppermute(first, 'depth', down(groups))  3.71 us
    ppermute x1, starting transfers between devices, on_device(): swap0 = lax.ppermute(jnp.where(c_odd, colfirst, collast), 'cols', inner)  2.09 us
    ppermute x1, starting transfers between devices, on_device(): before = lax.ppermute(last, 'depth', up(groups))  1.73 us
    pallas_call x1, Pallas kernels, on_device(): pl.pallas_call(strength_kernel, in_specs=[pl.BlockSpec(memory_space=pltpu...  1.72 us
    pallas_call x1, Pallas kernels, on_device(): pl.pallas_call(functools.partial(finish_kernel, step), out_shape=f32(rows...  1.1 us
    pallas_call x1, Pallas kernels, on_device(): pl.pallas_call(combine_kernel, out_shape=f32(4, SUB, lanes), compiler_par...  0.63 us
  transfers between devices with their start and end apart: 4, of which 0 were waited for; matrix products, arithmetic and copies ran while one was open for 0% of the time, Pallas kernels for 14%

profile of v3, /device:TPU:0, one launch (start us, length us, event | category | flops | bytes accessed | tf_op | source)
XLA Modules:
  0.0 27.1 jit_solution(6324335990612713198)
XLA Ops:
  0.0 1.7 %strength.1 = (f32[8,144,128]{2,1,0:T(8,128)S(1)}, f32[128,128]{1,0:T(8,128)S(1)}, f32[128,128]{1,0:T(8,128)S(1)}, f32[8,128]{1,0:T(8,128)S(1)}, f32[8,128]{1,0:...) custom-call(bf16[5,8,128,128]{3,2,1,0:T(8,128)(2,1)} %q_ref.1, s32[8,128,128]{2,1,0:T(8,128)} %lab_ref.1, ...), custom_call_target="tpu_custom_call" | custom-call | tf_op jit(solution)/shard_map/strength/pallas_call | solution.py:183
  1.7 1.7 %collective-permute-start = (f32[128,128]{1,0:T(8,128)S(1)}, f32[128,128]{1,0:T(8,128)S(1)}, u32[]{:S(2)}, u32[]{:S(2)}) collective-permute-start(f32[128,128]{1,0:T(8,128)S(1)} %get-tuple-element.23), channel_id=1, source_target_pairs={{0,1},{1,2},{2,3},{3,4},{4,5},{5,6},{6,7},{7,8},{8,9},{9,10},{10,1... | collective-permute-start | bytes 196616 | tf_op jit(solution)/shard_map/ppermute | solution.py:205
  3.5 3.7 %collective-permute-start.3 = (f32[128,128]{1,0:T(8,128)S(1)}, f32[128,128]{1,0:T(8,128)S(1)}, u32[]{:S(2)}, u32[]{:S(2)}) collective-permute-start(f32[128,128]{1,0:T(8,128)S(1)} %get-tuple-element.24), channel_id=1, source_target_pairs={{0,15},{1,0},{2,1},{3,2},{4,3},{5,4},{6,5},{7,6},{8,7},{9,8},{10,9... | collective-permute-start | bytes 196616 | tf_op jit(solution)/shard_map/ppermute | solution.py:204
  7.2 0.0 collective-permute-start.1
  7.2 2.1 %collective-permute-start.2 = (f32[8,128]{1,0:T(8,128)S(1)}, f32[8,128]{1,0:T(8,128)S(1)}, u32[]{:S(2)}, u32[]{:S(2)}) collective-permute-start(f32[8,128]{1,0:T(8,128)S(1)} %get-tuple-element.25), channel_id=1, source_target_pairs={{0,16},{16,0},{32,48},{48,32},{64,80},{80,64},{96,112},{112,96},{1... | collective-permute-start | bytes 12296 | tf_op jit(solution)/shard_map/ppermute | solution.py:213
  9.3 3.8 %lookup.1 = (f32[4,8,128,128]{3,2,1,0:T(8,128)S(1)}, f32[8,128,128]{2,1,0:T(8,128)S(1)}, f32[128,128]{1,0:T(8,128)S(1)}) custom-call(f32[2,8,128]{2,1,0:T(8,128)S(1)} %get-tuple-element.15.knots_ref, f32[8,144,128]{2,1,0:T(8,128)S(1)} %get-tuple-element.16.s_ref, s32[8,128,128]{2,1,0:T(8,128)S(1)} %get-tuple-element.17.lab_ref), custom_call_target="tpu_custom_call" | custom-call | flops 7864320 | bytes 3670016 | tf_op jit(solution)/shard_map/lookup/pallas_call | solution.py:216
  13.1 0.0 collective-permute-done.1.swap1_ref
  13.1 0.0 collective-permute-done.2.swap0_ref
  13.1 0.0 collective-permute-done.before_ref
  13.1 0.0 collective-permute-done.3.after_ref
  13.1 1.1 %finish.1 = f32[16,4,8,128]{3,2,1,0:T(8,128)S(1)} custom-call(f32[4,8,128,128]{3,2,1,0:T(8,128)S(1)} %get-tuple-element.18.value_ref, f32[8,128,128]{2,1,0:T(8,128)S(1)} %get-tuple-element.19.part_ref, f32[128,128]{1,0:T(8,128)S(1)} %get-tuple-element.20.edge_ref, f32[8,144,128]{2,1,0:T(8,128)S(1)} %get-tuple-element.16.s_ref, ...), custom_call_target="tpu_custom_call" | custom-call | tf_op jit(solution)/shard_map/finish/pallas_call | solution.py:224
  14.2 12.2 %all_to_all.5.slab_ref = f32[16,4,8,128]{3,2,1,0:T(8,128)S(1)} all-to-all(f32[16,4,8,128]{3,2,1,0:T(8,128)S(1)} %finish.1), channel_id=1, replica_groups=mesh['cols'=8,'depth'=16] {'depth'}, dimensions={0} | all-to-all | bytes 524288 | tf_op jit(solution)/shard_map/all_to_all | solution.py:232
  26.4 0.6 %combine.1 = f32[4,8,128]{2,1,0:T(8,128)} custom-call(f32[16,4,8,128]{3,2,1,0:T(8,128)S(1)} %all_to_all.5.slab_ref), custom_call_target="tpu_custom_call" | custom-call | tf_op jit(solution)/shard_map/combine/pallas_call | solution.py:233
  (1 shorter events, 0.0 us)
Async XLA Ops:
  1.7 11.4 %collective-permute-start = (f32[128,128]{1,0:T(8,128)S(1)}, f32[128,128]{1,0:T(8,128)S(1)}, u32[]{:S(2)}, u32[]{:S(2)}) collective-permute-start(f32[128,128]{1,0:T(8,128)S(1)} %get-tuple-element.23), channel_id=1, source_target_pairs={{0,1},{1,2},{2,3},{3,4},{4,5},{5,6},{6,7},{7,8},{8,9},{9,10},{10,1... | collective-permute-start | bytes 196616 | tf_op jit(solution)/shard_map/ppermute | solution.py:205
  3.5 9.7 %collective-permute-start.3 = (f32[128,128]{1,0:T(8,128)S(1)}, f32[128,128]{1,0:T(8,128)S(1)}, u32[]{:S(2)}, u32[]{:S(2)}) collective-permute-start(f32[128,128]{1,0:T(8,128)S(1)} %get-tuple-element.24), channel_id=1, source_target_pairs={{0,15},{1,0},{2,1},{3,2},{4,3},{5,4},{6,5},{7,6},{8,7},{9,8},{10,9... | collective-permute-start | bytes 196616 | tf_op jit(solution)/shard_map/ppermute | solution.py:204
  7.2 5.9 %collective-permute-start.1 = (f32[8,128]{1,0:T(8,128)S(1)}, f32[8,128]{1,0:T(8,128)S(1)}, u32[]{:S(2)}, u32[]{:S(2)}) collective-permute-start(f32[8,128]{1,0:T(8,128)S(1)} %get-tuple-element.26), channel_id=1, source_target_pairs={{0,1},{1,0},{2,3},{3,2},{4,5},{5,4},{6,7},{7,6},{8,9},{9,8},{10,11... | collective-permute-start | bytes 12296 | tf_op jit(solution)/shard_map/ppermute | solution.py:214
  7.2 5.9 %collective-permute-start.2 = (f32[8,128]{1,0:T(8,128)S(1)}, f32[8,128]{1,0:T(8,128)S(1)}, u32[]{:S(2)}, u32[]{:S(2)}) collective-permute-start(f32[8,128]{1,0:T(8,128)S(1)} %get-tuple-element.25), channel_id=1, source_target_pairs={{0,16},{16,0},{32,48},{48,32},{64,80},{80,64},{96,112},{112,96},{1... | collective-permute-start | bytes 12296 | tf_op jit(solution)/shard_map/ppermute | solution.py:213

commit v4 on v3

--- a/solution.py
+++ b/solution.py
@@ -10,9 +10,22 @@
 PAD = 8
 CHUNKS = 1
 BLOCK = 128
-
-
-def strength_kernel(q_ref, lab_ref, tab_ref, s_ref, first_ref, last_ref, colfirst_ref, collast_ref, lab_here, knots_ref, q_here, sems, tab_here, rows_tab, edge, edge_t):
+LEVELS = 65535.0
+MIDDLE = 32768
+MARGIN = 1.0001
+
+
+def encode(value, scale):
+    level = jnp.sqrt(jnp.clip(value / scale, 0.0, 1.0)) * LEVELS + 0.5
+    return level.astype(jnp.int32) - MIDDLE
+
+
+def decode(level, scale):
+    root = (level + MIDDLE).astype(jnp.float32) * (1.0 / LEVELS)
+    return root * root * scale
+
+
+def strength_kernel(step, q_ref, lab_ref, tab_ref, s_ref, first_ref, last_ref, colfirst_ref, collast_ref, lab_here, knots_ref, scale_ref, q_here, sems, tab_here, rows_tab, edge, edge_t):
     _, nz, rows, lanes = q_here.shape
     part = nz // CHUNKS
     copies = []
@@ -40,6 +53,10 @@
         knots = knots + pltpu.roll(rows_tab[lab], lab * nbins, 1)
     knots_ref[0] = knots
     knots_ref[1] = pltpu.roll(knots, lanes - 1, 1) - knots
+    top = jnp.broadcast_to(jnp.max(knots, axis=1, keepdims=True), (SUB, lanes))
+    cover = 1.0 - jnp.exp(-1.25 * step * nz * top[nchan - 1:nchan, :])
+    row = lax.broadcasted_iota(jnp.int32, (SUB, lanes), 0)
+    scale_ref[...] = jnp.where(row < nchan - 1, top, 1.0) * cover * MARGIN
 
     for k in range(CHUNKS):
         copies[k].wait()
@@ -106,7 +123,7 @@
     lax.fori_loop(0, rows // SUB, block, 0)
 
 
-def finish_kernel(step, value_ref, part_ref, edge_ref, s_ref, colfirst_ref, collast_ref, before_ref, swap1_ref, swap0_ref, after_ref,
+def finish_kernel(step, scale_ref, value_ref, part_ref, edge_ref, s_ref, colfirst_ref, collast_ref, before_ref, swap1_ref, swap0_ref, after_ref,
                   out_ref, halo, halo_t):
     _, nz, rows, lanes = value_ref.shape
     d = lax.axis_index("depth")
@@ -124,6 +141,8 @@
     halo[pl.ds(0, nz, stride=2), :] = right * has_right - colfirst_ref[...]
     halo[pl.ds(1, nz, stride=2), :] = collast_ref[...] - left * has_left
     halo_t[...] = halo[...].T
+
+    scale = [jnp.broadcast_to(scale_ref[k:k + 1, :], (SUB, lanes)) for k in range(4)]
 
     def block(i, carry):
         r0 = pl.multiple_of(i * SUB, SUB)
@@ -147,22 +166,25 @@
             for chan in range(3):
                 colors[chan] = colors[chan] + weight * value_ref[chan, z, at, :]
             transmit = passed
+        sent = [encode(v, scale[k]) for k, v in enumerate(colors + [1.0 - transmit])]
+        out_ref[i, 0] = jnp.concatenate(sent[:2], axis=0).astype(jnp.int16)
+        out_ref[i, 1] = jnp.concatenate(sent[2:], axis=0).astype(jnp.int16)
+        return carry
+
+    lax.fori_loop(0, rows // SUB, block, 0, unroll=8)
+
+
+def combine_kernel(scale_ref, slab_ref, out_ref):
+    count, _, _, lanes = slab_ref.shape
+    scale = [jnp.broadcast_to(scale_ref[k:k + 1, :], (SUB, lanes)) for k in range(4)]
+    transmit = jnp.ones((SUB, lanes), jnp.float32)
+    colors = [jnp.zeros((SUB, lanes), jnp.float32)] * 3
+    for k in range(count):
+        pairs = [slab_ref[k, j].astype(jnp.int32) for j in range(2)]
+        came = [decode(pairs[c // 2][c % 2 * SUB:(c % 2 + 1) * SUB], scale[c]) for c in range(4)]
         for chan in range(3):
-            out_ref[i, chan] = colors[chan]
-        out_ref[i, 3] = transmit
-        return carry
-
-    lax.fori_loop(0, rows // SUB, block, 0, unroll=2)
-
-
-def combine_kernel(slab_ref, out_ref):
-    count = slab_ref.shape[0]
-    transmit = slab_ref[0, 3]
-    colors = [slab_ref[0, chan] for chan in range(3)]
-    for k in range(1, count):
-        for chan in range(3):
-            colors[chan] = colors[chan] + transmit * slab_ref[k, chan]
-        transmit = transmit * slab_ref[k, 3]
+            colors[chan] = colors[chan] + transmit * came[chan]
+        transmit = transmit * (1.0 - came[3])
     for chan in range(3):
         out_ref[chan] = colors[chan]
     out_ref[3] = 1.0 - transmit
@@ -180,12 +202,12 @@
     plane = pltpu.VMEM((rows, lanes), jnp.float32)
     nlab, nchan, nbins = tables.shape
     far = lambda array: pltpu.with_memory_space_constraint(array, pltpu.HBM)
-    s, first, last, colfirst, collast, labels, knots = pl.pallas_call(
-        strength_kernel,
+    s, first, last, colfirst, collast, labels, knots, scale = pl.pallas_call(
+        functools.partial(strength_kernel, step),
         in_specs=[pl.BlockSpec(memory_space=pltpu.HBM)] * 3,
         out_shape=[
             f32(nz, rows + 2 * PAD, lanes), layer, layer, column, column,
-            jax.ShapeDtypeStruct(labels.shape, labels.dtype), f32(2, SUB, lanes),
+            jax.ShapeDtypeStruct(labels.shape, labels.dtype), f32(2, SUB, lanes), f32(SUB, lanes),
         ],
         scratch_shapes=[
             pltpu.VMEM(qtensor.shape, qtensor.dtype),
@@ -223,16 +245,16 @@
 
     slabs = pl.pallas_call(
         functools.partial(finish_kernel, step),
-        out_shape=f32(rows // SUB, 4, SUB, lanes),
+        out_shape=jax.ShapeDtypeStruct((rows // SUB, 2, 2 * SUB, lanes), jnp.int16),
         scratch_shapes=[pltpu.VMEM((lanes, rows), jnp.float32), plane],
         compiler_params=params,
         name="finish",
-    )(value, part, edge, s, colfirst, collast, before, swap1, swap0, after)
+    )(scale, value, part, edge, s, colfirst, collast, before, swap1, swap0, after)
 
     mine = lax.all_to_all(slabs, "depth", 0, 0)
     return pl.pallas_call(
         combine_kernel, out_shape=f32(4, SUB, lanes), compiler_params=params, name="combine"
-    )(mine)
+    )(scale, mine)
 
 
 def solution(mesh):

time: 27.2 us -> 26.1 us (0.960)
  blocking collectives: 12.2 us -> 11.4 us
  Pallas kernels: 7.27 us -> 6.98 us
    all_to_all x1, blocking collectives: 12.2 us -> 11.4 us  [on_device(): mine = lax.all_to_all(slabs, 'depth', 0, 0)]
    pallas_call x2, Pallas kernels: 2.82 us -> 2.48 us  [the longest x1 1.74 us: on_device(): pl.pallas_call(functools.partial(strength_kernel, step), in_specs=[pl.Blo...]
  transfers between devices with their start and end apart: 4 -> 4, of which waited for: 0 -> 0; matrix products, arithmetic and copies ran while one was open for 0% -> 0% of each run, Pallas kernels for 14% -> 15%
where the time goes in v4:
time: 26.1 us; the launch traced here: 25.9 us
  blocking collectives  11.4 us (44%)
  starting transfers between devices  7.53 us (29%)
  Pallas kernels  6.98 us (27%)
    all_to_all x1, blocking collectives, on_device(): mine = lax.all_to_all(slabs, 'depth', 0, 0)  11.4 us
    pallas_call x1, Pallas kernels, on_device(): pl.pallas_call(functools.partial(lookup_kernel, nbins), out_shape=[f32(nc...  3.82 us
    ppermute x1, starting transfers between devices, on_device(): after = lax.ppermute(first, 'depth', down(groups))  3.71 us
    ppermute x1, starting transfers between devices, on_device(): swap0 = lax.ppermute(jnp.where(c_odd, colfirst, collast), 'cols', inner)  2.09 us
    pallas_call x1, Pallas kernels, on_device(): pl.pallas_call(functools.partial(strength_kernel, step), in_specs=[pl.Blo...  1.74 us
    ppermute x1, starting transfers between devices, on_device(): before = lax.ppermute(last, 'depth', up(groups))  1.73 us
    pallas_call x1, Pallas kernels, on_device(): pl.pallas_call(functools.partial(finish_kernel, step), out_shape=jax.Shap...  0.74 us
    pallas_call x1, Pallas kernels, on_device(): pl.pallas_call(combine_kernel, out_shape=f32(4, SUB, lanes), compiler_par...  0.68 us
  transfers between devices with their start and end apart: 4, of which 0 were waited for; matrix products, arithmetic and copies ran while one was open for 0% of the time, Pallas kernels for 15%

profile of v4, /device:TPU:0, one launch (start us, length us, event | category | flops | bytes accessed | tf_op | source)
XLA Modules:
  0.0 25.9 jit_solution(16336393608379576170)
XLA Ops:
  0.0 1.7 %strength.1 = (f32[8,144,128]{2,1,0:T(8,128)S(1)}, f32[128,128]{1,0:T(8,128)S(1)}, f32[128,128]{1,0:T(8,128)S(1)}, f32[8,128]{1,0:T(8,128)S(1)}, f32[8,128]{1,0:...) custom-call(bf16[5,8,128,128]{3,2,1,0:T(8,128)(2,1)} %q_ref.1, ...), custom_call_target="tpu_custom_call" | custom-call | tf_op jit(solution)/shard_map/strength/pallas_call | solution.py:205
  1.7 1.7 %collective-permute-start = (f32[128,128]{1,0:T(8,128)S(1)}, f32[128,128]{1,0:T(8,128)S(1)}, u32[]{:S(2)}, u32[]{:S(2)}) collective-permute-start(f32[128,128]{1,0:T(8,128)S(1)} %get-tuple-element.25), channel_id=1, source_target_pairs={{0,1},{1,2},{2,3},{3,4},{4,5},{5,6},{6,7},{7,8},{8,9},{9,10},{10,1... | collective-permute-start | bytes 196616 | tf_op jit(solution)/shard_map/ppermute | solution.py:227
  3.5 3.7 %collective-permute-start.3 = (f32[128,128]{1,0:T(8,128)S(1)}, f32[128,128]{1,0:T(8,128)S(1)}, u32[]{:S(2)}, u32[]{:S(2)}) collective-permute-start(f32[128,128]{1,0:T(8,128)S(1)} %get-tuple-element.26), channel_id=1, source_target_pairs={{0,15},{1,0},{2,1},{3,2},{4,3},{5,4},{6,5},{7,6},{8,7},{9,8},{10,9... | collective-permute-start | bytes 196616 | tf_op jit(solution)/shard_map/ppermute | solution.py:226
  7.2 0.0 collective-permute-start.1
  7.2 2.1 %collective-permute-start.2 = (f32[8,128]{1,0:T(8,128)S(1)}, f32[8,128]{1,0:T(8,128)S(1)}, u32[]{:S(2)}, u32[]{:S(2)}) collective-permute-start(f32[8,128]{1,0:T(8,128)S(1)} %get-tuple-element.27), channel_id=1, source_target_pairs={{0,16},{16,0},{32,48},{48,32},{64,80},{80,64},{96,112},{112,96},{1... | collective-permute-start | bytes 12296 | tf_op jit(solution)/shard_map/ppermute | solution.py:235
  9.3 3.8 %lookup.1 = (f32[4,8,128,128]{3,2,1,0:T(8,128)S(1)}, f32[8,128,128]{2,1,0:T(8,128)S(1)}, f32[128,128]{1,0:T(8,128)S(1)}) custom-call(f32[2,8,128]{2,1,0:T(8,128)S(1)} %get-tuple-element.17.knots_ref, f32[8,144,128]{2,1,0:T(8,128)S(1)} %get-tuple-element.18.s_ref, s32[8,128,128]{2,1,0:T(8,128)S(1)} %get-tuple-element.19.lab_ref), custom_call_target="tpu_custom_call" | custom-call | flops 7864320 | bytes 3670016 | tf_op jit(solution)/shard_map/lookup/pallas_call | solution.py:238
  13.1 0.0 collective-permute-done.1.swap1_ref
  13.1 0.0 collective-permute-done.2.swap0_ref
  13.1 0.0 collective-permute-done.before_ref
  13.1 0.0 collective-permute-done.3.after_ref
  13.2 0.7 %finish.1 = s16[16,2,16,128]{3,2,1,0:T(8,128)(2,1)S(1)} custom-call(f32[8,128]{1,0:T(8,128)S(1)} %get-tuple-element.16.scale_ref, f32[4,8,128,128]{3,2,1,0:T(8,128)S(1)} %get-tuple-element.20.value_ref, f32[8,128,128]{2,1,0:T(8,128)S(1)} %get-tuple-element.21.part_ref, f32[128,128]{1,0:T(8,128)S(1)} %get-tuple-element.22.edge_ref, ...), custom_call_target="tpu_custom_call" | custom-call | tf_op jit(solution)/shard_map/finish/pallas_call | solution.py:246
  13.9 11.4 %all_to_all.5.slab_ref = s16[16,2,16,128]{3,2,1,0:T(8,128)(2,1)S(1)} all-to-all(s16[16,2,16,128]{3,2,1,0:T(8,128)(2,1)S(1)} %finish.1), channel_id=1, replica_groups=mesh['cols'=8,'depth'=16] {'depth'}, dimensions={0} | all-to-all | bytes 262144 | tf_op jit(solution)/shard_map/all_to_all | solution.py:254
  25.3 0.7 %combine.1 = f32[4,8,128]{2,1,0:T(8,128)} custom-call(f32[8,128]{1,0:T(8,128)S(1)} %get-tuple-element.16.scale_ref, s16[16,2,16,128]{3,2,1,0:T(8,128)(2,1)S(1)} %all_to_all.5.slab_ref), custom_call_target="tpu_custom_call" | custom-call | tf_op jit(solution)/shard_map/combine/pallas_call | solution.py:255
  (1 shorter events, 0.0 us)
Async XLA Ops:
  1.7 11.4 %collective-permute-start = (f32[128,128]{1,0:T(8,128)S(1)}, f32[128,128]{1,0:T(8,128)S(1)}, u32[]{:S(2)}, u32[]{:S(2)}) collective-permute-start(f32[128,128]{1,0:T(8,128)S(1)} %get-tuple-element.25), channel_id=1, source_target_pairs={{0,1},{1,2},{2,3},{3,4},{4,5},{5,6},{6,7},{7,8},{8,9},{9,10},{10,1... | collective-permute-start | bytes 196616 | tf_op jit(solution)/shard_map/ppermute | solution.py:227
  3.5 9.7 %collective-permute-start.3 = (f32[128,128]{1,0:T(8,128)S(1)}, f32[128,128]{1,0:T(8,128)S(1)}, u32[]{:S(2)}, u32[]{:S(2)}) collective-permute-start(f32[128,128]{1,0:T(8,128)S(1)} %get-tuple-element.26), channel_id=1, source_target_pairs={{0,15},{1,0},{2,1},{3,2},{4,3},{5,4},{6,5},{7,6},{8,7},{9,8},{10,9... | collective-permute-start | bytes 196616 | tf_op jit(solution)/shard_map/ppermute | solution.py:226
  7.2 5.9 %collective-permute-start.1 = (f32[8,128]{1,0:T(8,128)S(1)}, f32[8,128]{1,0:T(8,128)S(1)}, u32[]{:S(2)}, u32[]{:S(2)}) collective-permute-start(f32[8,128]{1,0:T(8,128)S(1)} %get-tuple-element.28), channel_id=1, source_target_pairs={{0,1},{1,0},{2,3},{3,2},{4,5},{5,4},{6,7},{7,6},{8,9},{9,8},{10,11... | collective-permute-start | bytes 12296 | tf_op jit(solution)/shard_map/ppermute | solution.py:236
  7.2 5.9 %collective-permute-start.2 = (f32[8,128]{1,0:T(8,128)S(1)}, f32[8,128]{1,0:T(8,128)S(1)}, u32[]{:S(2)}, u32[]{:S(2)}) collective-permute-start(f32[8,128]{1,0:T(8,128)S(1)} %get-tuple-element.27), channel_id=1, source_target_pairs={{0,16},{16,0},{32,48},{48,32},{64,80},{80,64},{96,112},{112,96},{1... | collective-permute-start | bytes 12296 | tf_op jit(solution)/shard_map/ppermute | solution.py:235

commit v5 on v4

--- a/solution.py
+++ b/solution.py
@@ -25,7 +25,7 @@
     return root * root * scale
 
 
-def strength_kernel(step, q_ref, lab_ref, tab_ref, s_ref, first_ref, last_ref, colfirst_ref, collast_ref, lab_here, knots_ref, scale_ref, q_here, sems, tab_here, rows_tab, edge, edge_t):
+def strength_kernel(step, q_ref, lab_ref, tab_ref, s_ref, first_ref, last_ref, colfirst_ref, collast_ref, lab_here, knots_ref, scale_ref, pick_ref, q_here, sems, tab_here, rows_tab, edge, edge_t):
     _, nz, rows, lanes = q_here.shape
     part = nz // CHUNKS
     copies = []
@@ -58,6 +58,16 @@
     row = lax.broadcasted_iota(jnp.int32, (SUB, lanes), 0)
     scale_ref[...] = jnp.where(row < nchan - 1, top, 1.0) * cover * MARGIN
 
+    src = lax.broadcasted_iota(jnp.int32, (lanes, 2 * lanes), 0)
+    dst = lax.broadcasted_iota(jnp.int32, (lanes, 2 * lanes), 1)
+    inside = (dst > 0) & (dst < lanes - 1)
+    near = jnp.where(inside & (src == dst + 1), 1.0, 0.0) - jnp.where(inside & (src == dst - 1), 1.0, 0.0)
+    odd = (dst & 1) == 1
+    ends = jnp.where(odd & (src == 1), 1.0, 0.0) - jnp.where(odd, 0.0, jnp.where(src == lanes - 2, 1.0, 0.0))
+    pick = jnp.where(dst < lanes, near, ends).astype(jnp.bfloat16)
+    pick_ref[0:lanes, :] = pick
+    pick_ref[lanes:, :] = pick
+
     for k in range(CHUNKS):
         copies[k].wait()
 
@@ -84,26 +94,33 @@
     lab_copy.wait()
 
 
-def lookup_kernel(nbins, knots_ref, s_ref, lab_ref, value_ref, part_ref, edge_ref):
+def lookup_kernel(nbins, knots_ref, pick_ref, s_ref, lab_ref, value_ref, part_ref, edge_ref, dx_here):
     nz, rows, lanes = lab_ref.shape
     nchan = value_ref.shape[0]
-    lane = lax.broadcasted_iota(jnp.int32, (SUB, lanes), 1)
-    inner = (lane > 0) & (lane < lanes - 1)
+    lane = lax.broadcasted_iota(jnp.int32, (rows, lanes), 1)
     base = [jnp.broadcast_to(knots_ref[0, k:k + 1, :], (SUB, lanes)) for k in range(nchan)]
     diff = [jnp.broadcast_to(knots_ref[1, k:k + 1, :], (SUB, lanes)) for k in range(nchan)]
+
+    packed = jnp.zeros((rows, lanes), jnp.float32)
+    for z in range(nz):
+        layer = s_ref[z, PAD:PAD + rows, :]
+        high = layer.astype(jnp.bfloat16)
+        low = (layer - high.astype(jnp.float32)).astype(jnp.bfloat16)
+        both = jnp.dot(jnp.concatenate([high, low], axis=1), pick_ref[...], preferred_element_type=jnp.float32)
+        dx_here[z] = both[:, :lanes]
+        packed = jnp.where(lane >> 1 == z, both[:, lanes:], packed)
+    edge_ref[...] = packed
 
     def block(i, carry):
         r0 = pl.multiple_of(i * SUB, SUB)
         at = pl.ds(r0, SUB)
-        packed = jnp.zeros((SUB, lanes), jnp.float32)
         below = None
         here = s_ref[0, pl.ds(r0 + PAD, SUB), :]
         for z in range(nz):
             above = s_ref[z + 1, pl.ds(r0 + PAD, SUB), :] if z < nz - 1 else None
-            dx = pltpu.roll(here, lanes - 1, 1) - pltpu.roll(here, 1, 1)
-            packed = jnp.where(lane >> 1 == z, pltpu.roll(dx, 2 * z + 1, 1), packed)
+            dx = dx_here[z, at, :]
             dy = s_ref[z, pl.ds(r0 + PAD + 1, SUB), :] - s_ref[z, pl.ds(r0 + PAD - 1, SUB), :]
-            part = dy * dy + jnp.where(inner, dx * dx, 0.0)
+            part = dy * dy + dx * dx
             if 0 < z < nz - 1:
                 dz = above - below
                 part = part + dz * dz
@@ -117,13 +134,12 @@
                 rise = jnp.take_along_axis(diff[chan], index, axis=1, mode="promise_in_bounds")
                 value_ref[chan, z, at, :] = low + frac * rise
             below, here = here, above
-        edge_ref[at, :] = packed
         return carry
 
     lax.fori_loop(0, rows // SUB, block, 0)
 
 
-def finish_kernel(step, scale_ref, value_ref, part_ref, edge_ref, s_ref, colfirst_ref, collast_ref, before_ref, swap1_ref, swap0_ref, after_ref,
+def finish_kernel(step, scale_ref, value_ref, part_ref, edge_ref, s_ref, before_ref, swap1_ref, swap0_ref, after_ref,
                   out_ref, halo, halo_t):
     _, nz, rows, lanes = value_ref.shape
     d = lax.axis_index("depth")
@@ -138,8 +154,8 @@
     odd = c % 2 == 1
     left = jnp.where(odd, swap0_ref[...], swap1_ref[...])
     right = jnp.where(odd, swap1_ref[...], swap0_ref[...])
-    halo[pl.ds(0, nz, stride=2), :] = right * has_right - colfirst_ref[...]
-    halo[pl.ds(1, nz, stride=2), :] = collast_ref[...] - left * has_left
+    halo[pl.ds(0, nz, stride=2), :] = right * has_right
+    halo[pl.ds(1, nz, stride=2), :] = -left * has_left
     halo_t[...] = halo[...].T
 
     scale = [jnp.broadcast_to(scale_ref[k:k + 1, :], (SUB, lanes)) for k in range(4)]
@@ -202,12 +218,13 @@
     plane = pltpu.VMEM((rows, lanes), jnp.float32)
     nlab, nchan, nbins = tables.shape
     far = lambda array: pltpu.with_memory_space_constraint(array, pltpu.HBM)
-    s, first, last, colfirst, collast, labels, knots, scale = pl.pallas_call(
+    s, first, last, colfirst, collast, labels, knots, scale, pick = pl.pallas_call(
         functools.partial(strength_kernel, step),
         in_specs=[pl.BlockSpec(memory_space=pltpu.HBM)] * 3,
         out_shape=[
             f32(nz, rows + 2 * PAD, lanes), layer, layer, column, column,
             jax.ShapeDtypeStruct(labels.shape, labels.dtype), f32(2, SUB, lanes), f32(SUB, lanes),
+            jax.ShapeDtypeStruct((2 * lanes, 2 * lanes), jnp.bfloat16),
         ],
         scratch_shapes=[
             pltpu.VMEM(qtensor.shape, qtensor.dtype),
@@ -238,10 +255,11 @@
     value, part, edge = pl.pallas_call(
         functools.partial(lookup_kernel, nbins),
         out_shape=[f32(nchan, nz, rows, lanes), f32(nz, rows, lanes), layer],
+        scratch_shapes=[pltpu.VMEM((nz, rows, lanes), jnp.float32)],
         compiler_params=params,
         cost_estimate=pl.CostEstimate(flops=60 * nz * rows * lanes, bytes_accessed=28 * nz * rows * lanes, transcendentals=0),
         name="lookup",
-    )(knots, s, labels)
+    )(knots, pick, s, labels)
 
     slabs = pl.pallas_call(
         functools.partial(finish_kernel, step),
@@ -249,7 +267,7 @@
         scratch_shapes=[pltpu.VMEM((lanes, rows), jnp.float32), plane],
         compiler_params=params,
         name="finish",
-    )(scale, value, part, edge, s, colfirst, collast, before, swap1, swap0, after)
+    )(scale, value, part, edge, s, before, swap1, swap0, after)
 
     mine = lax.all_to_all(slabs, "depth", 0, 0)
     return pl.pallas_call(

time: 26.1 us -> 25.4 us (0.973)
  starting transfers between devices: 7.53 us -> 5.45 us
  blocking collectives: 11.4 us -> 13 us
  Pallas kernels: 6.98 us -> 6.2 us
  waiting for transfers between devices: 0.01 us -> 0.54 us
    ppermute x1, starting transfers between devices: 2.09 us -> 0.01 us  [on_device(): swap0 = lax.ppermute(jnp.where(c_odd, colfirst, collast), 'cols', inner)]
    all_to_all x1, blocking collectives: 11.4 us -> 13 us  [on_device(): mine = lax.all_to_all(slabs, 'depth', 0, 0)]
    pallas_call x1, Pallas kernels: 3.82 us -> 3.05 us  [on_device(): pl.pallas_call(functools.partial(lookup_kernel, nbins), out_shape=[f32(nc...]
    ppermute x1, waiting for transfers between devices: 0.01 us -> 0.54 us  [on_device(): lax.ppermute(jnp.where(c_odd, collast, colfirst), ('cols', 'depth'), outer)]
  transfers between devices with their start and end apart: 4 -> 4, of which waited for: 0 -> 1; matrix products, arithmetic and copies ran while one was open for 0% -> 0% of each run, Pallas kernels for 15% -> 12%
where the time goes in v5:
time: 25.4 us; the launch traced here: 25.2 us
  blocking collectives  13 us (51%)
  Pallas kernels  6.2 us (24%)
  starting transfers between devices  5.45 us (21%)
  waiting for transfers between devices  0.54 us (2%)
    all_to_all x1, blocking collectives, on_device(): mine = lax.all_to_all(slabs, 'depth', 0, 0)  13 us
    ppermute x1, starting transfers between devices, on_device(): after = lax.ppermute(first, 'depth', down(groups))  3.71 us
    pallas_call x1, Pallas kernels, on_device(): pl.pallas_call(functools.partial(lookup_kernel, nbins), out_shape=[f32(nc...  3.05 us
    pallas_call x1, Pallas kernels, on_device(): pl.pallas_call(functools.partial(strength_kernel, step), in_specs=[pl.Blo...  1.74 us
    ppermute x1, starting transfers between devices, on_device(): before = lax.ppermute(last, 'depth', up(groups))  1.73 us
    pallas_call x1, Pallas kernels, on_device(): pl.pallas_call(functools.partial(finish_kernel, step), out_shape=jax.Shap...  0.73 us
    pallas_call x1, Pallas kernels, on_device(): pl.pallas_call(combine_kernel, out_shape=f32(4, SUB, lanes), compiler_par...  0.68 us
    ppermute x1, waiting for transfers between devices, on_device(): lax.ppermute(jnp.where(c_odd, collast, colfirst), ('cols', 'depth'), outer)  0.54 us
  transfers between devices with their start and end apart: 4, of which 1 were waited for; matrix products, arithmetic and copies ran while one was open for 0% of the time, Pallas kernels for 12%

profile of v5, /device:TPU:0, one launch (start us, length us, event | category | flops | bytes accessed | tf_op | source)
XLA Modules:
  0.0 25.2 jit_solution(10125704672320608926)
XLA Ops:
  0.0 1.7 %strength.1 = (f32[8,144,128]{2,1,0:T(8,128)S(1)}, f32[128,128]{1,0:T(8,128)S(1)}, f32[128,128]{1,0:T(8,128)S(1)}, f32[8,128]{1,0:T(8,128)S(1)}, f32[8,128]{1,0:...) custom-call(bf16[5,8,128,128]{3,2,1,0:T(8,128)(2,1)} %q_ref.1, ...), custom_call_target="tpu_custom_call" | custom-call | tf_op jit(solution)/shard_map/strength/pallas_call | solution.py:221
  1.7 1.7 %collective-permute-start = (f32[128,128]{1,0:T(8,128)S(1)}, f32[128,128]{1,0:T(8,128)S(1)}, u32[]{:S(2)}, u32[]{:S(2)}) collective-permute-start(f32[128,128]{1,0:T(8,128)S(1)} %get-tuple-element.25), channel_id=1, source_target_pairs={{0,1},{1,2},{2,3},{3,4},{4,5},{5,6},{6,7},{7,8},{8,9},{9,10},{10,1... | collective-permute-start | bytes 196616 | tf_op jit(solution)/shard_map/ppermute | solution.py:244
  3.5 3.7 %collective-permute-start.3 = (f32[128,128]{1,0:T(8,128)S(1)}, f32[128,128]{1,0:T(8,128)S(1)}, u32[]{:S(2)}, u32[]{:S(2)}) collective-permute-start(f32[128,128]{1,0:T(8,128)S(1)} %get-tuple-element.28), channel_id=1, source_target_pairs={{0,15},{1,0},{2,1},{3,2},{4,3},{5,4},{6,5},{7,6},{8,7},{9,8},{10,9... | collective-permute-start | bytes 196616 | tf_op jit(solution)/shard_map/ppermute | solution.py:243
  7.2 0.0 collective-permute-start.2
  7.2 0.0 collective-permute-start.1
  7.2 3.0 %lookup.1 = (f32[4,8,128,128]{3,2,1,0:T(8,128)S(1)}, f32[8,128,128]{2,1,0:T(8,128)S(1)}, f32[128,128]{1,0:T(8,128)S(1)}) custom-call(f32[2,8,128]{2,1,0:T(8,128)S(1)} %get-tuple-element.18.knots_ref, bf16[256,256]{1,0:T(8,128)(2,1)S(1)} %get-tuple-element.19.pick_ref, f32[8,144,128]{2,1,0:T(8,128)S(1)} %get-tuple-element.20.s_ref, ...), custom_call_target="tpu_custom_call" | custom-call | flops 7864320 | bytes 3670016 | tf_op jit(solution)/shard_map/lookup/pallas_call | solution.py:255
  10.3 0.0 collective-permute-done.2.swap0_ref
  10.3 0.5 %collective-permute-done.1.swap1_ref = f32[8,128]{1,0:T(8,128)S(1)} collective-permute-done((f32[8,128]{1,0:T(8,128)S(1)}, f32[8,128]{1,0:T(8,128)S(1)}, u32[]{:S(2)}, u32[]{:S(2)}) %collective-permute-start.1) | collective-permute-done | bytes 4128 | tf_op jit(solution)/shard_map/ppermute | solution.py:253
  10.8 0.0 collective-permute-done.before_ref
  10.8 0.0 collective-permute-done.3.after_ref
  10.8 0.7 %finish.1 = s16[16,2,16,128]{3,2,1,0:T(8,128)(2,1)S(1)} custom-call(f32[8,128]{1,0:T(8,128)S(1)} %get-tuple-element.17.scale_ref, f32[4,8,128,128]{3,2,1,0:T(8,128)S(1)} %get-tuple-element.22.value_ref, f32[8,128,128]{2,1,0:T(8,128)S(1)} %get-tuple-element.23.part_ref, f32[128,128]{1,0:T(8,128)S(1)} %get-tuple-element.24.edge_ref, ...), custom_call_target="tpu_custom_call" | custom-call | tf_op jit(solution)/shard_map/finish/pallas_call | solution.py:264
  11.6 13.0 %all_to_all.5.slab_ref = s16[16,2,16,128]{3,2,1,0:T(8,128)(2,1)S(1)} all-to-all(s16[16,2,16,128]{3,2,1,0:T(8,128)(2,1)S(1)} %finish.1), channel_id=1, replica_groups=mesh['cols'=8,'depth'=16] {'depth'}, dimensions={0} | all-to-all | bytes 262144 | tf_op jit(solution)/shard_map/all_to_all | solution.py:272
  24.5 0.7 %combine.1 = f32[4,8,128]{2,1,0:T(8,128)} custom-call(f32[8,128]{1,0:T(8,128)S(1)} %get-tuple-element.17.scale_ref, s16[16,2,16,128]{3,2,1,0:T(8,128)(2,1)S(1)} %all_to_all.5.slab_ref), custom_call_target="tpu_custom_call" | custom-call | tf_op jit(solution)/shard_map/combine/pallas_call | solution.py:273
  (1 shorter events, 0.0 us)
Async XLA Ops:
  1.7 9.1 %collective-permute-start = (f32[128,128]{1,0:T(8,128)S(1)}, f32[128,128]{1,0:T(8,128)S(1)}, u32[]{:S(2)}, u32[]{:S(2)}) collective-permute-start(f32[128,128]{1,0:T(8,128)S(1)} %get-tuple-element.25), channel_id=1, source_target_pairs={{0,1},{1,2},{2,3},{3,4},{4,5},{5,6},{6,7},{7,8},{8,9},{9,10},{10,1... | collective-permute-start | bytes 196616 | tf_op jit(solution)/shard_map/ppermute | solution.py:244
  3.5 7.3 %collective-permute-start.3 = (f32[128,128]{1,0:T(8,128)S(1)}, f32[128,128]{1,0:T(8,128)S(1)}, u32[]{:S(2)}, u32[]{:S(2)}) collective-permute-start(f32[128,128]{1,0:T(8,128)S(1)} %get-tuple-element.28), channel_id=1, source_target_pairs={{0,15},{1,0},{2,1},{3,2},{4,3},{5,4},{6,5},{7,6},{8,7},{9,8},{10,9... | collective-permute-start | bytes 196616 | tf_op jit(solution)/shard_map/ppermute | solution.py:243
  7.2 3.1 %collective-permute-start.2 = (f32[8,128]{1,0:T(8,128)S(1)}, f32[8,128]{1,0:T(8,128)S(1)}, u32[]{:S(2)}, u32[]{:S(2)}) collective-permute-start(f32[8,128]{1,0:T(8,128)S(1)} %get-tuple-element.29), channel_id=1, source_target_pairs={{0,16},{16,0},{32,48},{48,32},{64,80},{80,64},{96,112},{112,96},{1... | collective-permute-start | bytes 12296 | tf_op jit(solution)/shard_map/ppermute | solution.py:252
  7.2 3.6 %collective-permute-start.1 = (f32[8,128]{1,0:T(8,128)S(1)}, f32[8,128]{1,0:T(8,128)S(1)}, u32[]{:S(2)}, u32[]{:S(2)}) collective-permute-start(f32[8,128]{1,0:T(8,128)S(1)} %get-tuple-element.30), channel_id=1, source_target_pairs={{0,1},{1,0},{2,3},{3,2},{4,5},{5,4},{6,7},{7,6},{8,9},{9,8},{10,11... | collective-permute-start | bytes 12296 | tf_op jit(solution)/shard_map/ppermute | solution.py:253

commit v6 on v5

--- a/solution.py
+++ b/solution.py
@@ -13,6 +13,7 @@
 LEVELS = 65535.0
 MIDDLE = 32768
 MARGIN = 1.0001
+STRENGTH_MAX = 3.0 * 6.0 * 2.5 * 2.5 * MARGIN
 
 
 def encode(value, scale):
@@ -79,9 +80,9 @@
                 s = 3.0 * (q[0] * q[0] + q[3] * q[3] + q[0] * q[3] + q[1] * q[1] + q[2] * q[2] + q[4] * q[4])
                 s_ref[z, pl.ds(r0 + PAD, BLOCK), :] = s
                 if z == 0:
-                    first_ref[pl.ds(r0, BLOCK), :] = s
+                    first_ref[pl.ds(r0, BLOCK), :] = encode(s, STRENGTH_MAX).astype(jnp.int16)
                 if z == nz - 1:
-                    last_ref[pl.ds(r0, BLOCK), :] = s
+                    last_ref[pl.ds(r0, BLOCK), :] = encode(s, STRENGTH_MAX).astype(jnp.int16)
                 turned = pltpu.roll(s, 2 * z + 1, 1)
                 packed = jnp.where(lane >> 1 == z, turned, packed)
             edge[pl.ds(r0, BLOCK), :] = packed
@@ -140,7 +141,7 @@
 
 
 def finish_kernel(step, scale_ref, value_ref, part_ref, edge_ref, s_ref, before_ref, swap1_ref, swap0_ref, after_ref,
-                  out_ref, halo, halo_t):
+                  out_ref, halo, halo_t, below_here, above_here):
     _, nz, rows, lanes = value_ref.shape
     d = lax.axis_index("depth")
     c = lax.axis_index("cols")
@@ -157,6 +158,8 @@
     halo[pl.ds(0, nz, stride=2), :] = right * has_right
     halo[pl.ds(1, nz, stride=2), :] = -left * has_left
     halo_t[...] = halo[...].T
+    below_here[...] = decode(before_ref[...].astype(jnp.int32), STRENGTH_MAX) * has_before
+    above_here[...] = decode(after_ref[...].astype(jnp.int32), STRENGTH_MAX) * has_after
 
     scale = [jnp.broadcast_to(scale_ref[k:k + 1, :], (SUB, lanes)) for k in range(4)]
 
@@ -171,10 +174,10 @@
         for z in range(nz):
             slope4 = part_ref[z, at, :] + jnp.where(outer, pltpu.roll(sides, lanes - 1 - 2 * z, 1), 0.0)
             if z == 0:
-                dz = s_ref[1, inside, :] - before_ref[at, :] * has_before
+                dz = s_ref[1, inside, :] - below_here[at, :]
                 slope4 = slope4 + dz * dz
             if z == nz - 1:
-                dz = after_ref[at, :] * has_after - s_ref[nz - 2, inside, :]
+                dz = above_here[at, :] - s_ref[nz - 2, inside, :]
                 slope4 = slope4 + dz * dz
             extinction = value_ref[3, z, at, :] * (1.25 - 4.0 / (4.0 + slope4))
             passed = transmit * jnp.exp(-step * extinction)
@@ -214,6 +217,7 @@
     params = pltpu.CompilerParams(vmem_limit_bytes=32 * 1024 * 1024)
     f32 = lambda *shape: jax.ShapeDtypeStruct(shape, jnp.float32)
     layer = f32(rows, lanes)
+    coded = jax.ShapeDtypeStruct((rows, lanes), jnp.int16)
     column = f32(nz, rows)
     plane = pltpu.VMEM((rows, lanes), jnp.float32)
     nlab, nchan, nbins = tables.shape
@@ -222,7 +226,7 @@
         functools.partial(strength_kernel, step),
         in_specs=[pl.BlockSpec(memory_space=pltpu.HBM)] * 3,
         out_shape=[
-            f32(nz, rows + 2 * PAD, lanes), layer, layer, column, column,
+            f32(nz, rows + 2 * PAD, lanes), coded, coded, column, column,
             jax.ShapeDtypeStruct(labels.shape, labels.dtype), f32(2, SUB, lanes), f32(SUB, lanes),
             jax.ShapeDtypeStruct((2 * lanes, 2 * lanes), jnp.bfloat16),
         ],
@@ -264,7 +268,7 @@
     slabs = pl.pallas_call(
         functools.partial(finish_kernel, step),
         out_shape=jax.ShapeDtypeStruct((rows // SUB, 2, 2 * SUB, lanes), jnp.int16),
-        scratch_shapes=[pltpu.VMEM((lanes, rows), jnp.float32), plane],
+        scratch_shapes=[pltpu.VMEM((lanes, rows), jnp.float32), plane, plane, plane],
         compiler_params=params,
         name="finish",
     )(scale, value, part, edge, s, before, swap1, swap0, after)

time: 25.4 us -> 25.1 us (0.988)
  blocking collectives: 13 us -> 12.6 us
    all_to_all x1, blocking collectives: 13 us -> 12.6 us  [on_device(): mine = lax.all_to_all(slabs, 'depth', 0, 0)]
where the time goes in v6:
time: 25.1 us; the launch traced here: 24.9 us
  blocking collectives  12.6 us (50%)
  Pallas kernels  6.27 us (25%)
  starting transfers between devices  5.45 us (22%)
  waiting for transfers between devices  0.54 us (2%)
    all_to_all x1, blocking collectives, on_device(): mine = lax.all_to_all(slabs, 'depth', 0, 0)  12.6 us
    ppermute x1, starting transfers between devices, on_device(): after = lax.ppermute(first, 'depth', down(groups))  3.71 us
    pallas_call x1, Pallas kernels, on_device(): pl.pallas_call(functools.partial(lookup_kernel, nbins), out_shape=[f32(nc...  3.05 us
    pallas_call x1, Pallas kernels, on_device(): pl.pallas_call(functools.partial(strength_kernel, step), in_specs=[pl.Blo...  1.79 us
    ppermute x1, starting transfers between devices, on_device(): before = lax.ppermute(last, 'depth', up(groups))  1.73 us
    pallas_call x1, Pallas kernels, on_device(): pl.pallas_call(functools.partial(finish_kernel, step), out_shape=jax.Shap...  0.75 us
    pallas_call x1, Pallas kernels, on_device(): pl.pallas_call(combine_kernel, out_shape=f32(4, SUB, lanes), compiler_par...  0.68 us
    ppermute x1, waiting for transfers between devices, on_device(): lax.ppermute(jnp.where(c_odd, collast, colfirst), ('cols', 'depth'), outer)  0.54 us
  transfers between devices with their start and end apart: 4, of which 1 were waited for; matrix products, arithmetic and copies ran while one was open for 0% of the time, Pallas kernels for 12%

profile of v6, /device:TPU:0, one launch (start us, length us, event | category | flops | bytes accessed | tf_op | source)
XLA Modules:
  0.0 24.9 jit_solution(4723456305020661263)
XLA Ops:
  0.0 1.8 %strength.1 = (f32[8,144,128]{2,1,0:T(8,128)S(1)}, s16[128,128]{1,0:T(8,128)(2,1)S(1)}, s16[128,128]{1,0:T(8,128)(2,1)S(1)}, f32[8,128]{1,0:T(8,128)S(1)}, f32[8...) custom-call(bf16[5,8,128,128]{3,2,1,0:T(8,128)(2,1)} %q_ref.1, ...), custom_call_target="tpu_custom_call" | custom-call | tf_op jit(solution)/shard_map/strength/pallas_call | solution.py:225
  1.8 1.7 %collective-permute-start = (s16[128,128]{1,0:T(8,128)(2,1)S(1)}, s16[128,128]{1,0:T(8,128)(2,1)S(1)}, u32[]{:S(2)}, u32[]{:S(2)}) collective-permute-start(s16[128,128]{1,0:T(8,128)(2,1)S(1)} %get-tuple-element.25), channel_id=1, source_target_pairs={{0,1},{1,2},{2,3},{3,4},{4,5},{5,6},{6,7},{7,8},{8,9},{9,10},{10,1... | collective-permute-start | bytes 98312 | tf_op jit(solution)/shard_map/ppermute | solution.py:248
  3.5 3.7 %collective-permute-start.3 = (s16[128,128]{1,0:T(8,128)(2,1)S(1)}, s16[128,128]{1,0:T(8,128)(2,1)S(1)}, u32[]{:S(2)}, u32[]{:S(2)}) collective-permute-start(s16[128,128]{1,0:T(8,128)(2,1)S(1)} %get-tuple-element.28), channel_id=1, source_target_pairs={{0,15},{1,0},{2,1},{3,2},{4,3},{5,4},{6,5},{7,6},{8,7},{9,8},{10,9... | collective-permute-start | bytes 98312 | tf_op jit(solution)/shard_map/ppermute | solution.py:247
  7.2 0.0 collective-permute-start.2
  7.2 0.0 collective-permute-start.1
  7.3 3.0 %lookup.1 = (f32[4,8,128,128]{3,2,1,0:T(8,128)S(1)}, f32[8,128,128]{2,1,0:T(8,128)S(1)}, f32[128,128]{1,0:T(8,128)S(1)}) custom-call(f32[2,8,128]{2,1,0:T(8,128)S(1)} %get-tuple-element.18.knots_ref, bf16[256,256]{1,0:T(8,128)(2,1)S(1)} %get-tuple-element.19.pick_ref, f32[8,144,128]{2,1,0:T(8,128)S(1)} %get-tuple-element.20.s_ref, ...), custom_call_target="tpu_custom_call" | custom-call | flops 7864320 | bytes 3670016 | tf_op jit(solution)/shard_map/lookup/pallas_call | solution.py:259
  10.3 0.0 collective-permute-done.2.swap0_ref
  10.3 0.5 %collective-permute-done.1.swap1_ref = f32[8,128]{1,0:T(8,128)S(1)} collective-permute-done((f32[8,128]{1,0:T(8,128)S(1)}, f32[8,128]{1,0:T(8,128)S(1)}, u32[]{:S(2)}, u32[]{:S(2)}) %collective-permute-start.1) | collective-permute-done | bytes 4128 | tf_op jit(solution)/shard_map/ppermute | solution.py:257
  10.9 0.0 collective-permute-done.before_ref
  10.9 0.0 collective-permute-done.3.after_ref
  10.9 0.8 %finish.1 = s16[16,2,16,128]{3,2,1,0:T(8,128)(2,1)S(1)} custom-call(f32[8,128]{1,0:T(8,128)S(1)} %get-tuple-element.17.scale_ref, f32[4,8,128,128]{3,2,1,0:T(8,128)S(1)} %get-tuple-element.22.value_ref, f32[8,128,128]{2,1,0:T(8,128)S(1)} %get-tuple-element.23.part_ref, f32[128,128]{1,0:T(8,128)S(1)} %get-tuple-element.24.edge_ref, ...), custom_call_target="tpu_custom_call" | custom-call | tf_op jit(solution)/shard_map/finish/pallas_call | solution.py:268
  11.6 12.6 %all_to_all.5.slab_ref = s16[16,2,16,128]{3,2,1,0:T(8,128)(2,1)S(1)} all-to-all(s16[16,2,16,128]{3,2,1,0:T(8,128)(2,1)S(1)} %finish.1), channel_id=1, replica_groups=mesh['cols'=8,'depth'=16] {'depth'}, dimensions={0} | all-to-all | bytes 262144 | tf_op jit(solution)/shard_map/all_to_all | solution.py:276
  24.3 0.7 %combine.1 = f32[4,8,128]{2,1,0:T(8,128)} custom-call(f32[8,128]{1,0:T(8,128)S(1)} %get-tuple-element.17.scale_ref, s16[16,2,16,128]{3,2,1,0:T(8,128)(2,1)S(1)} %all_to_all.5.slab_ref), custom_call_target="tpu_custom_call" | custom-call | tf_op jit(solution)/shard_map/combine/pallas_call | solution.py:277
  (1 shorter events, 0.0 us)
Async XLA Ops:
  1.8 9.1 %collective-permute-start = (s16[128,128]{1,0:T(8,128)(2,1)S(1)}, s16[128,128]{1,0:T(8,128)(2,1)S(1)}, u32[]{:S(2)}, u32[]{:S(2)}) collective-permute-start(s16[128,128]{1,0:T(8,128)(2,1)S(1)} %get-tuple-element.25), channel_id=1, source_target_pairs={{0,1},{1,2},{2,3},{3,4},{4,5},{5,6},{6,7},{7,8},{8,9},{9,10},{10,1... | collective-permute-start | bytes 98312 | tf_op jit(solution)/shard_map/ppermute | solution.py:248
  3.5 7.3 %collective-permute-start.3 = (s16[128,128]{1,0:T(8,128)(2,1)S(1)}, s16[128,128]{1,0:T(8,128)(2,1)S(1)}, u32[]{:S(2)}, u32[]{:S(2)}) collective-permute-start(s16[128,128]{1,0:T(8,128)(2,1)S(1)} %get-tuple-element.28), channel_id=1, source_target_pairs={{0,15},{1,0},{2,1},{3,2},{4,3},{5,4},{6,5},{7,6},{8,7},{9,8},{10,9... | collective-permute-start | bytes 98312 | tf_op jit(solution)/shard_map/ppermute | solution.py:247
  7.2 3.1 %collective-permute-start.2 = (f32[8,128]{1,0:T(8,128)S(1)}, f32[8,128]{1,0:T(8,128)S(1)}, u32[]{:S(2)}, u32[]{:S(2)}) collective-permute-start(f32[8,128]{1,0:T(8,128)S(1)} %get-tuple-element.29), channel_id=1, source_target_pairs={{0,16},{16,0},{32,48},{48,32},{64,80},{80,64},{96,112},{112,96},{1... | collective-permute-start | bytes 12296 | tf_op jit(solution)/shard_map/ppermute | solution.py:256
  7.2 3.6 %collective-permute-start.1 = (f32[8,128]{1,0:T(8,128)S(1)}, f32[8,128]{1,0:T(8,128)S(1)}, u32[]{:S(2)}, u32[]{:S(2)}) collective-permute-start(f32[8,128]{1,0:T(8,128)S(1)} %get-tuple-element.30), channel_id=1, source_target_pairs={{0,1},{1,0},{2,3},{3,2},{4,5},{5,4},{6,7},{7,6},{8,9},{9,8},{10,11... | collective-permute-start | bytes 12296 | tf_op jit(solution)/shard_map/ppermute | solution.py:257

commit v7 on v6

--- a/solution.py
+++ b/solution.py
@@ -8,7 +8,7 @@
 
 SUB = 8
 PAD = 8
-CHUNKS = 1
+CHUNKS = 2
 BLOCK = 128
 LEVELS = 65535.0
 MIDDLE = 32768
@@ -28,14 +28,14 @@
 
 def strength_kernel(step, q_ref, lab_ref, tab_ref, s_ref, first_ref, last_ref, colfirst_ref, collast_ref, lab_here, knots_ref, scale_ref, pick_ref, q_here, sems, tab_here, rows_tab, edge, edge_t):
     _, nz, rows, lanes = q_here.shape
+    tab_copy = pltpu.make_async_copy(tab_ref, tab_here, sems.at[CHUNKS])
+    tab_copy.start()
     part = nz // CHUNKS
     copies = []
     for k in range(CHUNKS):
         at = pl.ds(k * part, part)
         copies.append(pltpu.make_async_copy(q_ref.at[:, at], q_here.at[:, at], sems.at[k]))
         copies[k].start()
-    tab_copy = pltpu.make_async_copy(tab_ref, tab_here, sems.at[CHUNKS])
-    tab_copy.start()
     lab_copy = pltpu.make_async_copy(lab_ref, lab_here, sems.at[CHUNKS + 1])
     lab_copy.start()
     lane = lax.broadcasted_iota(jnp.int32, (BLOCK, lanes), 1)
@@ -43,6 +43,16 @@
     for z in range(nz):
         s_ref[z, 0:PAD, :] = zeros
         s_ref[z, PAD + rows:, :] = zeros
+
+    src = lax.broadcasted_iota(jnp.int32, (lanes, 2 * lanes), 0)
+    dst = lax.broadcasted_iota(jnp.int32, (lanes, 2 * lanes), 1)
+    inside = (dst > 0) & (dst < lanes - 1)
+    near = jnp.where(inside & (src == dst + 1), 1.0, 0.0) - jnp.where(inside & (src == dst - 1), 1.0, 0.0)
+    odd = (dst & 1) == 1
+    ends = jnp.where(odd & (src == 1), 1.0, 0.0) - jnp.where(odd, 0.0, jnp.where(src == lanes - 2, 1.0, 0.0))
+    pick = jnp.where(dst < lanes, near, ends).astype(jnp.bfloat16)
+    pick_ref[0:lanes, :] = pick
+    pick_ref[lanes:, :] = pick
 
     nlab, nchan, nbins = tab_here.shape
     rows_tab[...] = jnp.zeros_like(rows_tab)
@@ -58,16 +68,6 @@
     cover = 1.0 - jnp.exp(-1.25 * step * nz * top[nchan - 1:nchan, :])
     row = lax.broadcasted_iota(jnp.int32, (SUB, lanes), 0)
     scale_ref[...] = jnp.where(row < nchan - 1, top, 1.0) * cover * MARGIN
-
-    src = lax.broadcasted_iota(jnp.int32, (lanes, 2 * lanes), 0)
-    dst = lax.broadcasted_iota(jnp.int32, (lanes, 2 * lanes), 1)
-    inside = (dst > 0) & (dst < lanes - 1)
-    near = jnp.where(inside & (src == dst + 1), 1.0, 0.0) - jnp.where(inside & (src == dst - 1), 1.0, 0.0)
-    odd = (dst & 1) == 1
-    ends = jnp.where(odd & (src == 1), 1.0, 0.0) - jnp.where(odd, 0.0, jnp.where(src == lanes - 2, 1.0, 0.0))
-    pick = jnp.where(dst < lanes, near, ends).astype(jnp.bfloat16)
-    pick_ref[0:lanes, :] = pick
-    pick_ref[lanes:, :] = pick
 
     for k in range(CHUNKS):
         copies[k].wait()

time: 25.1 us -> 24.9 us (level)
  no operation moved by 1% of the time
where the time goes in v7:
time: 24.9 us; the launch traced here: 24.8 us
  blocking collectives  12.6 us (51%)
  Pallas kernels  6.1 us (24%)
  starting transfers between devices  5.45 us (22%)
  waiting for transfers between devices  0.54 us (2%)
    all_to_all x1, blocking collectives, on_device(): mine = lax.all_to_all(slabs, 'depth', 0, 0)  12.6 us
    ppermute x1, starting transfers between devices, on_device(): after = lax.ppermute(first, 'depth', down(groups))  3.71 us
    pallas_call x1, Pallas kernels, on_device(): pl.pallas_call(functools.partial(lookup_kernel, nbins), out_shape=[f32(nc...  3.05 us
    ppermute x1, starting transfers between devices, on_device(): before = lax.ppermute(last, 'depth', up(groups))  1.73 us
    pallas_call x1, Pallas kernels, on_device(): pl.pallas_call(functools.partial(strength_kernel, step), in_specs=[pl.Blo...  1.62 us
    pallas_call x1, Pallas kernels, on_device(): pl.pallas_call(functools.partial(finish_kernel, step), out_shape=jax.Shap...  0.75 us
    pallas_call x1, Pallas kernels, on_device(): pl.pallas_call(combine_kernel, out_shape=f32(4, SUB, lanes), compiler_par...  0.68 us
    ppermute x1, waiting for transfers between devices, on_device(): lax.ppermute(jnp.where(c_odd, collast, colfirst), ('cols', 'depth'), outer)  0.54 us
  transfers between devices with their start and end apart: 4, of which 1 were waited for; matrix products, arithmetic and copies ran while one was open for 0% of the time, Pallas kernels for 12%

profile of v7, /device:TPU:0, one launch (start us, length us, event | category | flops | bytes accessed | tf_op | source)
XLA Modules:
  0.0 24.8 jit_solution(14100892791811562204)
XLA Ops:
  0.0 1.6 %strength.1 = (f32[8,144,128]{2,1,0:T(8,128)S(1)}, s16[128,128]{1,0:T(8,128)(2,1)S(1)}, s16[128,128]{1,0:T(8,128)(2,1)S(1)}, f32[8,128]{1,0:T(8,128)S(1)}, f32[8...) custom-call(bf16[5,8,128,128]{3,2,1,0:T(8,128)(2,1)} %q_ref.1, ...), custom_call_target="tpu_custom_call" | custom-call | tf_op jit(solution)/shard_map/strength/pallas_call | solution.py:225
  1.6 1.7 %collective-permute-start = (s16[128,128]{1,0:T(8,128)(2,1)S(1)}, s16[128,128]{1,0:T(8,128)(2,1)S(1)}, u32[]{:S(2)}, u32[]{:S(2)}) collective-permute-start(s16[128,128]{1,0:T(8,128)(2,1)S(1)} %get-tuple-element.25), channel_id=1, source_target_pairs={{0,1},{1,2},{2,3},{3,4},{4,5},{5,6},{6,7},{7,8},{8,9},{9,10},{10,1... | collective-permute-start | bytes 98312 | tf_op jit(solution)/shard_map/ppermute | solution.py:248
  3.4 3.7 %collective-permute-start.3 = (s16[128,128]{1,0:T(8,128)(2,1)S(1)}, s16[128,128]{1,0:T(8,128)(2,1)S(1)}, u32[]{:S(2)}, u32[]{:S(2)}) collective-permute-start(s16[128,128]{1,0:T(8,128)(2,1)S(1)} %get-tuple-element.28), channel_id=1, source_target_pairs={{0,15},{1,0},{2,1},{3,2},{4,3},{5,4},{6,5},{7,6},{8,7},{9,8},{10,9... | collective-permute-start | bytes 98312 | tf_op jit(solution)/shard_map/ppermute | solution.py:247
  7.1 0.0 collective-permute-start.2
  7.1 0.0 collective-permute-start.1
  7.1 3.0 %lookup.1 = (f32[4,8,128,128]{3,2,1,0:T(8,128)S(1)}, f32[8,128,128]{2,1,0:T(8,128)S(1)}, f32[128,128]{1,0:T(8,128)S(1)}) custom-call(f32[2,8,128]{2,1,0:T(8,128)S(1)} %get-tuple-element.18.knots_ref, bf16[256,256]{1,0:T(8,128)(2,1)S(1)} %get-tuple-element.19.pick_ref, f32[8,144,128]{2,1,0:T(8,128)S(1)} %get-tuple-element.20.s_ref, ...), custom_call_target="tpu_custom_call" | custom-call | flops 7864320 | bytes 3670016 | tf_op jit(solution)/shard_map/lookup/pallas_call | solution.py:259
  10.1 0.0 collective-permute-done.2.swap0_ref
  10.2 0.5 %collective-permute-done.1.swap1_ref = f32[8,128]{1,0:T(8,128)S(1)} collective-permute-done((f32[8,128]{1,0:T(8,128)S(1)}, f32[8,128]{1,0:T(8,128)S(1)}, u32[]{:S(2)}, u32[]{:S(2)}) %collective-permute-start.1) | collective-permute-done | bytes 4128 | tf_op jit(solution)/shard_map/ppermute | solution.py:257
  10.7 0.0 collective-permute-done.before_ref
  10.7 0.0 collective-permute-done.3.after_ref
  10.7 0.8 %finish.1 = s16[16,2,16,128]{3,2,1,0:T(8,128)(2,1)S(1)} custom-call(f32[8,128]{1,0:T(8,128)S(1)} %get-tuple-element.17.scale_ref, f32[4,8,128,128]{3,2,1,0:T(8,128)S(1)} %get-tuple-element.22.value_ref, f32[8,128,128]{2,1,0:T(8,128)S(1)} %get-tuple-element.23.part_ref, f32[128,128]{1,0:T(8,128)S(1)} %get-tuple-element.24.edge_ref, ...), custom_call_target="tpu_custom_call" | custom-call | tf_op jit(solution)/shard_map/finish/pallas_call | solution.py:268
  11.5 12.6 %all_to_all.5.slab_ref = s16[16,2,16,128]{3,2,1,0:T(8,128)(2,1)S(1)} all-to-all(s16[16,2,16,128]{3,2,1,0:T(8,128)(2,1)S(1)} %finish.1), channel_id=1, replica_groups=mesh['cols'=8,'depth'=16] {'depth'}, dimensions={0} | all-to-all | bytes 262144 | tf_op jit(solution)/shard_map/all_to_all | solution.py:276
  24.1 0.7 %combine.1 = f32[4,8,128]{2,1,0:T(8,128)} custom-call(f32[8,128]{1,0:T(8,128)S(1)} %get-tuple-element.17.scale_ref, s16[16,2,16,128]{3,2,1,0:T(8,128)(2,1)S(1)} %all_to_all.5.slab_ref), custom_call_target="tpu_custom_call" | custom-call | tf_op jit(solution)/shard_map/combine/pallas_call | solution.py:277
  (1 shorter events, 0.0 us)
Async XLA Ops:
  1.6 9.1 %collective-permute-start = (s16[128,128]{1,0:T(8,128)(2,1)S(1)}, s16[128,128]{1,0:T(8,128)(2,1)S(1)}, u32[]{:S(2)}, u32[]{:S(2)}) collective-permute-start(s16[128,128]{1,0:T(8,128)(2,1)S(1)} %get-tuple-element.25), channel_id=1, source_target_pairs={{0,1},{1,2},{2,3},{3,4},{4,5},{5,6},{6,7},{7,8},{8,9},{9,10},{10,1... | collective-permute-start | bytes 98312 | tf_op jit(solution)/shard_map/ppermute | solution.py:248
  3.4 7.3 %collective-permute-start.3 = (s16[128,128]{1,0:T(8,128)(2,1)S(1)}, s16[128,128]{1,0:T(8,128)(2,1)S(1)}, u32[]{:S(2)}, u32[]{:S(2)}) collective-permute-start(s16[128,128]{1,0:T(8,128)(2,1)S(1)} %get-tuple-element.28), channel_id=1, source_target_pairs={{0,15},{1,0},{2,1},{3,2},{4,3},{5,4},{6,5},{7,6},{8,7},{9,8},{10,9... | collective-permute-start | bytes 98312 | tf_op jit(solution)/shard_map/ppermute | solution.py:247
  7.1 3.1 %collective-permute-start.2 = (f32[8,128]{1,0:T(8,128)S(1)}, f32[8,128]{1,0:T(8,128)S(1)}, u32[]{:S(2)}, u32[]{:S(2)}) collective-permute-start(f32[8,128]{1,0:T(8,128)S(1)} %get-tuple-element.29), channel_id=1, source_target_pairs={{0,16},{16,0},{32,48},{48,32},{64,80},{80,64},{96,112},{112,96},{1... | collective-permute-start | bytes 12296 | tf_op jit(solution)/shard_map/ppermute | solution.py:256
  7.1 3.6 %collective-permute-start.1 = (f32[8,128]{1,0:T(8,128)S(1)}, f32[8,128]{1,0:T(8,128)S(1)}, u32[]{:S(2)}, u32[]{:S(2)}) collective-permute-start(f32[8,128]{1,0:T(8,128)S(1)} %get-tuple-element.30), channel_id=1, source_target_pairs={{0,1},{1,0},{2,3},{3,2},{4,5},{5,4},{6,7},{7,6},{8,9},{9,8},{10,11... | collective-permute-start | bytes 12296 | tf_op jit(solution)/shard_map/ppermute | solution.py:257

commit v8 on v7

--- a/solution.py
+++ b/solution.py
@@ -137,7 +137,7 @@
             below, here = here, above
         return carry
 
-    lax.fori_loop(0, rows // SUB, block, 0)
+    lax.fori_loop(0, rows // SUB, block, 0, unroll=4)
 
 
 def finish_kernel(step, scale_ref, value_ref, part_ref, edge_ref, s_ref, before_ref, swap1_ref, swap0_ref, after_ref,
@@ -190,7 +190,7 @@
         out_ref[i, 1] = jnp.concatenate(sent[2:], axis=0).astype(jnp.int16)
         return carry
 
-    lax.fori_loop(0, rows // SUB, block, 0, unroll=8)
+    lax.fori_loop(0, rows // SUB, block, 0, unroll=16)
 
 
 def combine_kernel(scale_ref, slab_ref, out_ref):
@@ -252,7 +252,7 @@
     for i in range(across):
         j = ((i + 1) ^ 1) - 1
         for g in range(groups):
-            outer.append((i * groups + g, j * groups + g if 0 <= j < across else i * groups + (g ^ 1)))
+            outer.append((i * groups + g, j * groups + g if 0 <= j < across else i * groups + (g ^ groups // 4)))
     swap0 = lax.ppermute(jnp.where(c_odd, colfirst, collast), "cols", inner)
     swap1 = lax.ppermute(jnp.where(c_odd, collast, colfirst), ("cols", "depth"), outer)
 

time: 24.9 us -> 24.8 us (level)
  Pallas kernels: 6.1 us -> 5.05 us
  waiting for transfers between devices: 0.54 us -> 1.16 us
  starting transfers between devices: 5.45 us -> 5.78 us
    pallas_call x1, Pallas kernels: 3.05 us -> 2.1 us  [on_device(): pl.pallas_call(functools.partial(lookup_kernel, nbins), out_shape=[f32(nc...]
    ppermute x1, waiting for transfers between devices: 0.54 us -> 1.16 us  [on_device(): lax.ppermute(jnp.where(c_odd, collast, colfirst), ('cols', 'depth'), outer)]
    ppermute x1, starting transfers between devices: 0.01 us -> 0.34 us  [on_device(): lax.ppermute(jnp.where(c_odd, collast, colfirst), ('cols', 'depth'), outer)]
  transfers between devices with their start and end apart: 4 -> 4, of which waited for: 1 -> 1; matrix products, arithmetic and copies ran while one was open for 0% -> 0% of each run, Pallas kernels for 12% -> 9%
where the time goes in v8:
time: 24.8 us; the launch traced here: 24.7 us
  blocking collectives  12.6 us (51%)
  starting transfers between devices  5.78 us (23%)
  Pallas kernels  5.05 us (20%)
  waiting for transfers between devices  1.16 us (5%)
    all_to_all x1, blocking collectives, on_device(): mine = lax.all_to_all(slabs, 'depth', 0, 0)  12.6 us
    ppermute x1, starting transfers between devices, on_device(): after = lax.ppermute(first, 'depth', down(groups))  3.71 us
    pallas_call x1, Pallas kernels, on_device(): pl.pallas_call(functools.partial(lookup_kernel, nbins), out_shape=[f32(nc...  2.1 us
    ppermute x1, starting transfers between devices, on_device(): before = lax.ppermute(last, 'depth', up(groups))  1.73 us
    pallas_call x1, Pallas kernels, on_device(): pl.pallas_call(functools.partial(strength_kernel, step), in_specs=[pl.Blo...  1.62 us
    ppermute x1, waiting for transfers between devices, on_device(): lax.ppermute(jnp.where(c_odd, collast, colfirst), ('cols', 'depth'), outer)  1.16 us
    pallas_call x1, Pallas kernels, on_device(): pl.pallas_call(combine_kernel, out_shape=f32(4, SUB, lanes), compiler_par...  0.68 us
    pallas_call x1, Pallas kernels, on_device(): pl.pallas_call(functools.partial(finish_kernel, step), out_shape=jax.Shap...  0.65 us
  transfers between devices with their start and end apart: 4, of which 1 were waited for; matrix products, arithmetic and copies ran while one was open for 0% of the time, Pallas kernels for 9%

profile of v8, /device:TPU:0, one launch (start us, length us, event | category | flops | bytes accessed | tf_op | source)
XLA Modules:
  0.0 24.7 jit_solution(3043647202862247176)
XLA Ops:
  0.0 1.6 %strength.1 = (f32[8,144,128]{2,1,0:T(8,128)S(1)}, s16[128,128]{1,0:T(8,128)(2,1)S(1)}, s16[128,128]{1,0:T(8,128)(2,1)S(1)}, f32[8,128]{1,0:T(8,128)S(1)}, f32[8...) custom-call(bf16[5,8,128,128]{3,2,1,0:T(8,128)(2,1)} %q_ref.1, ...), custom_call_target="tpu_custom_call" | custom-call | tf_op jit(solution)/shard_map/strength/pallas_call | solution.py:225
  1.6 1.7 %collective-permute-start = (s16[128,128]{1,0:T(8,128)(2,1)S(1)}, s16[128,128]{1,0:T(8,128)(2,1)S(1)}, u32[]{:S(2)}, u32[]{:S(2)}) collective-permute-start(s16[128,128]{1,0:T(8,128)(2,1)S(1)} %get-tuple-element.25), channel_id=1, source_target_pairs={{0,1},{1,2},{2,3},{3,4},{4,5},{5,6},{6,7},{7,8},{8,9},{9,10},{10,1... | collective-permute-start | bytes 98312 | tf_op jit(solution)/shard_map/ppermute | solution.py:248
  3.4 3.7 %collective-permute-start.3 = (s16[128,128]{1,0:T(8,128)(2,1)S(1)}, s16[128,128]{1,0:T(8,128)(2,1)S(1)}, u32[]{:S(2)}, u32[]{:S(2)}) collective-permute-start(s16[128,128]{1,0:T(8,128)(2,1)S(1)} %get-tuple-element.28), channel_id=1, source_target_pairs={{0,15},{1,0},{2,1},{3,2},{4,3},{5,4},{6,5},{7,6},{8,7},{9,8},{10,9... | collective-permute-start | bytes 98312 | tf_op jit(solution)/shard_map/ppermute | solution.py:247
  7.1 0.0 collective-permute-start.2
  7.1 0.3 %collective-permute-start.1 = (f32[8,128]{1,0:T(8,128)S(1)}, f32[8,128]{1,0:T(8,128)S(1)}, u32[]{:S(2)}, u32[]{:S(2)}) collective-permute-start(f32[8,128]{1,0:T(8,128)S(1)} %get-tuple-element.30), channel_id=1, source_target_pairs={{0,4},{1,5},{2,6},{3,7},{4,0},{5,1},{6,2},{7,3},{8,12},{9,13},{10,... | collective-permute-start | bytes 12296 | tf_op jit(solution)/shard_map/ppermute | solution.py:257
  7.4 2.1 %lookup.1 = (f32[4,8,128,128]{3,2,1,0:T(8,128)S(1)}, f32[8,128,128]{2,1,0:T(8,128)S(1)}, f32[128,128]{1,0:T(8,128)S(1)}) custom-call(f32[2,8,128]{2,1,0:T(8,128)S(1)} %get-tuple-element.18.knots_ref, bf16[256,256]{1,0:T(8,128)(2,1)S(1)} %get-tuple-element.19.pick_ref, f32[8,144,128]{2,1,0:T(8,128)S(1)} %get-tuple-element.20.s_ref, ...), custom_call_target="tpu_custom_call" | custom-call | flops 7864320 | bytes 3670016 | tf_op jit(solution)/shard_map/lookup/pallas_call | solution.py:259
  9.5 0.0 collective-permute-done.2.swap0_ref
  9.5 1.2 %collective-permute-done.1.swap1_ref = f32[8,128]{1,0:T(8,128)S(1)} collective-permute-done((f32[8,128]{1,0:T(8,128)S(1)}, f32[8,128]{1,0:T(8,128)S(1)}, u32[]{:S(2)}, u32[]{:S(2)}) %collective-permute-start.1) | collective-permute-done | bytes 4128 | tf_op jit(solution)/shard_map/ppermute | solution.py:257
  10.7 0.0 collective-permute-done.before_ref
  10.7 0.0 collective-permute-done.3.after_ref
  10.7 0.6 %finish.1 = s16[16,2,16,128]{3,2,1,0:T(8,128)(2,1)S(1)} custom-call(f32[8,128]{1,0:T(8,128)S(1)} %get-tuple-element.17.scale_ref, f32[4,8,128,128]{3,2,1,0:T(8,128)S(1)} %get-tuple-element.22.value_ref, f32[8,128,128]{2,1,0:T(8,128)S(1)} %get-tuple-element.23.part_ref, f32[128,128]{1,0:T(8,128)S(1)} %get-tuple-element.24.edge_ref, ...), custom_call_target="tpu_custom_call" | custom-call | tf_op jit(solution)/shard_map/finish/pallas_call | solution.py:268
  11.4 12.6 %all_to_all.5.slab_ref = s16[16,2,16,128]{3,2,1,0:T(8,128)(2,1)S(1)} all-to-all(s16[16,2,16,128]{3,2,1,0:T(8,128)(2,1)S(1)} %finish.1), channel_id=1, replica_groups=mesh['cols'=8,'depth'=16] {'depth'}, dimensions={0} | all-to-all | bytes 262144 | tf_op jit(solution)/shard_map/all_to_all | solution.py:276
  24.0 0.7 %combine.1 = f32[4,8,128]{2,1,0:T(8,128)} custom-call(f32[8,128]{1,0:T(8,128)S(1)} %get-tuple-element.17.scale_ref, s16[16,2,16,128]{3,2,1,0:T(8,128)(2,1)S(1)} %all_to_all.5.slab_ref), custom_call_target="tpu_custom_call" | custom-call | tf_op jit(solution)/shard_map/combine/pallas_call | solution.py:277
  (1 shorter events, 0.0 us)
Async XLA Ops:
  1.6 9.1 %collective-permute-start = (s16[128,128]{1,0:T(8,128)(2,1)S(1)}, s16[128,128]{1,0:T(8,128)(2,1)S(1)}, u32[]{:S(2)}, u32[]{:S(2)}) collective-permute-start(s16[128,128]{1,0:T(8,128)(2,1)S(1)} %get-tuple-element.25), channel_id=1, source_target_pairs={{0,1},{1,2},{2,3},{3,4},{4,5},{5,6},{6,7},{7,8},{8,9},{9,10},{10,1... | collective-permute-start | bytes 98312 | tf_op jit(solution)/shard_map/ppermute | solution.py:248
  3.4 7.3 %collective-permute-start.3 = (s16[128,128]{1,0:T(8,128)(2,1)S(1)}, s16[128,128]{1,0:T(8,128)(2,1)S(1)}, u32[]{:S(2)}, u32[]{:S(2)}) collective-permute-start(s16[128,128]{1,0:T(8,128)(2,1)S(1)} %get-tuple-element.28), channel_id=1, source_target_pairs={{0,15},{1,0},{2,1},{3,2},{4,3},{5,4},{6,5},{7,6},{8,7},{9,8},{10,9... | collective-permute-start | bytes 98312 | tf_op jit(solution)/shard_map/ppermute | solution.py:247
  7.1 2.4 %collective-permute-start.2 = (f32[8,128]{1,0:T(8,128)S(1)}, f32[8,128]{1,0:T(8,128)S(1)}, u32[]{:S(2)}, u32[]{:S(2)}) collective-permute-start(f32[8,128]{1,0:T(8,128)S(1)} %get-tuple-element.29), channel_id=1, source_target_pairs={{0,16},{16,0},{32,48},{48,32},{64,80},{80,64},{96,112},{112,96},{1... | collective-permute-start | bytes 12296 | tf_op jit(solution)/shard_map/ppermute | solution.py:256
  7.1 3.6 %collective-permute-start.1 = (f32[8,128]{1,0:T(8,128)S(1)}, f32[8,128]{1,0:T(8,128)S(1)}, u32[]{:S(2)}, u32[]{:S(2)}) collective-permute-start(f32[8,128]{1,0:T(8,128)S(1)} %get-tuple-element.30), channel_id=1, source_target_pairs={{0,4},{1,5},{2,6},{3,7},{4,0},{5,1},{6,2},{7,3},{8,12},{9,13},{10,... | collective-permute-start | bytes 12296 | tf_op jit(solution)/shard_map/ppermute | solution.py:257

commit v9 on v8

--- a/solution.py
+++ b/solution.py
@@ -140,13 +140,12 @@
     lax.fori_loop(0, rows // SUB, block, 0, unroll=4)
 
 
-def finish_kernel(step, scale_ref, value_ref, part_ref, edge_ref, s_ref, before_ref, swap1_ref, swap0_ref, after_ref,
-                  out_ref, halo, halo_t, below_here, above_here):
+def most_kernel(step, value_ref, part_ref, edge_ref, s_ref, before_ref, swap1_ref, swap0_ref,
+                state_ref, slope_ref, halo, halo_t, below_here):
     _, nz, rows, lanes = value_ref.shape
     d = lax.axis_index("depth")
     c = lax.axis_index("cols")
     has_before = (d > 0).astype(jnp.float32)
-    has_after = (d < lax.axis_size("depth") - 1).astype(jnp.float32)
     has_left = (c > 0).astype(jnp.float32)
     has_right = (c < lax.axis_size("cols") - 1).astype(jnp.float32)
     lane = lax.broadcasted_iota(jnp.int32, (SUB, lanes), 1)
@@ -159,9 +158,7 @@
     halo[pl.ds(1, nz, stride=2), :] = -left * has_left
     halo_t[...] = halo[...].T
     below_here[...] = decode(before_ref[...].astype(jnp.int32), STRENGTH_MAX) * has_before
-    above_here[...] = decode(after_ref[...].astype(jnp.int32), STRENGTH_MAX) * has_after
-
-    scale = [jnp.broadcast_to(scale_ref[k:k + 1, :], (SUB, lanes)) for k in range(4)]
+
 
     def block(i, carry):
         r0 = pl.multiple_of(i * SUB, SUB)
@@ -177,15 +174,38 @@
                 dz = s_ref[1, inside, :] - below_here[at, :]
                 slope4 = slope4 + dz * dz
             if z == nz - 1:
-                dz = above_here[at, :] - s_ref[nz - 2, inside, :]
-                slope4 = slope4 + dz * dz
+                slope_ref[at, :] = slope4
+                break
             extinction = value_ref[3, z, at, :] * (1.25 - 4.0 / (4.0 + slope4))
             passed = transmit * jnp.exp(-step * extinction)
             weight = transmit - passed
             for chan in range(3):
                 colors[chan] = colors[chan] + weight * value_ref[chan, z, at, :]
             transmit = passed
-        sent = [encode(v, scale[k]) for k, v in enumerate(colors + [1.0 - transmit])]
+        for k, v in enumerate(colors + [transmit]):
+            state_ref[i, k] = v
+        return carry
+
+    lax.fori_loop(0, rows // SUB, block, 0, unroll=16)
+
+
+def last_kernel(step, scale_ref, state_ref, slope_ref, value_ref, s_ref, after_ref, out_ref, above_here):
+    _, nz, rows, lanes = value_ref.shape
+    has_after = (lax.axis_index("depth") < lax.axis_size("depth") - 1).astype(jnp.float32)
+    above_here[...] = decode(after_ref[...].astype(jnp.int32), STRENGTH_MAX) * has_after
+    scale = [jnp.broadcast_to(scale_ref[k:k + 1, :], (SUB, lanes)) for k in range(4)]
+
+    def block(i, carry):
+        r0 = pl.multiple_of(i * SUB, SUB)
+        at = pl.ds(r0, SUB)
+        dz = above_here[at, :] - s_ref[nz - 2, pl.ds(r0 + PAD, SUB), :]
+        slope4 = slope_ref[at, :] + dz * dz
+        extinction = value_ref[3, nz - 1, at, :] * (1.25 - 4.0 / (4.0 + slope4))
+        transmit = state_ref[i, 3]
+        passed = transmit * jnp.exp(-step * extinction)
+        weight = transmit - passed
+        colors = [state_ref[i, chan] + weight * value_ref[chan, nz - 1, at, :] for chan in range(3)]
+        sent = [encode(v, scale[k]) for k, v in enumerate(colors + [1.0 - passed])]
         out_ref[i, 0] = jnp.concatenate(sent[:2], axis=0).astype(jnp.int16)
         out_ref[i, 1] = jnp.concatenate(sent[2:], axis=0).astype(jnp.int16)
         return carry
@@ -265,13 +285,20 @@
         name="lookup",
     )(knots, pick, s, labels)
 
+    state, slope = pl.pallas_call(
+        functools.partial(most_kernel, step),
+        out_shape=[f32(rows // SUB, 4, SUB, lanes), layer],
+        scratch_shapes=[pltpu.VMEM((lanes, rows), jnp.float32), plane, plane],
+        compiler_params=params,
+        name="most",
+    )(value, part, edge, s, before, swap1, swap0)
     slabs = pl.pallas_call(
-        functools.partial(finish_kernel, step),
+        functools.partial(last_kernel, step),
         out_shape=jax.ShapeDtypeStruct((rows // SUB, 2, 2 * SUB, lanes), jnp.int16),
-        scratch_shapes=[pltpu.VMEM((lanes, rows), jnp.float32), plane, plane, plane],
+        scratch_shapes=[plane],
         compiler_params=params,
-        name="finish",
-    )(scale, value, part, edge, s, before, swap1, swap0, after)
+        name="last",
+    )(scale, state, slope, value, s, after)
 
     mine = lax.all_to_all(slabs, "depth", 0, 0)
     return pl.pallas_call(

time: 24.8 us -> 24.4 us (0.984)
  blocking collectives: 12.6 us -> 12.2 us
    all_to_all x1, blocking collectives: 12.6 us -> 12.2 us  [on_device(): mine = lax.all_to_all(slabs, 'depth', 0, 0)]
    pallas_call x1 -> x2, Pallas kernels: 0.65 us -> 0.67 us  [the longest x1 0.46 us: on_device(): pl.pallas_call(functools.partial(most_kernel, step), out_shape=[f32(rows...]
  transfers between devices with their start and end apart: 4 -> 4, of which waited for: 1 -> 1; matrix products, arithmetic and copies ran while one was open for 0% -> 0% of each run, Pallas kernels for 9% -> 11%
where the time goes in v9:
time: 24.4 us; the launch traced here: 24.2 us
  blocking collectives  12.2 us (50%)
  starting transfers between devices  5.78 us (24%)
  Pallas kernels  5.07 us (21%)
  waiting for transfers between devices  1.16 us (5%)
    all_to_all x1, blocking collectives, on_device(): mine = lax.all_to_all(slabs, 'depth', 0, 0)  12.2 us
    ppermute x1, starting transfers between devices, on_device(): after = lax.ppermute(first, 'depth', down(groups))  3.71 us
    pallas_call x1, Pallas kernels, on_device(): pl.pallas_call(functools.partial(lookup_kernel, nbins), out_shape=[f32(nc...  2.1 us
    ppermute x1, starting transfers between devices, on_device(): before = lax.ppermute(last, 'depth', up(groups))  1.73 us
    pallas_call x1, Pallas kernels, on_device(): pl.pallas_call(functools.partial(strength_kernel, step), in_specs=[pl.Blo...  1.62 us
    ppermute x1, waiting for transfers between devices, on_device(): lax.ppermute(jnp.where(c_odd, collast, colfirst), ('cols', 'depth'), outer)  1.16 us
    pallas_call x1, Pallas kernels, on_device(): pl.pallas_call(combine_kernel, out_shape=f32(4, SUB, lanes), compiler_par...  0.68 us
  transfers between devices with their start and end apart: 4, of which 1 were waited for; matrix products, arithmetic and copies ran while one was open for 0% of the time, Pallas kernels for 11%

profile of v9, /device:TPU:0, one launch (start us, length us, event | category | flops | bytes accessed | tf_op | source)
XLA Modules:
  0.0 24.2 jit_solution(935330089984240233)
XLA Ops:
  0.0 1.6 %strength.1 = (f32[8,144,128]{2,1,0:T(8,128)S(1)}, s16[128,128]{1,0:T(8,128)(2,1)S(1)}, s16[128,128]{1,0:T(8,128)(2,1)S(1)}, f32[8,128]{1,0:T(8,128)S(1)}, f32[8...) custom-call(bf16[5,8,128,128]{3,2,1,0:T(8,128)(2,1)} %q_ref.1, ...), custom_call_target="tpu_custom_call" | custom-call | tf_op jit(solution)/shard_map/strength/pallas_call | solution.py:245
  1.6 1.7 %collective-permute-start = (s16[128,128]{1,0:T(8,128)(2,1)S(1)}, s16[128,128]{1,0:T(8,128)(2,1)S(1)}, u32[]{:S(2)}, u32[]{:S(2)}) collective-permute-start(s16[128,128]{1,0:T(8,128)(2,1)S(1)} %get-tuple-element.27), channel_id=1, source_target_pairs={{0,1},{1,2},{2,3},{3,4},{4,5},{5,6},{6,7},{7,8},{8,9},{9,10},{10,1... | collective-permute-start | bytes 98312 | tf_op jit(solution)/shard_map/ppermute | solution.py:268
  3.4 3.7 %collective-permute-start.3 = (s16[128,128]{1,0:T(8,128)(2,1)S(1)}, s16[128,128]{1,0:T(8,128)(2,1)S(1)}, u32[]{:S(2)}, u32[]{:S(2)}) collective-permute-start(s16[128,128]{1,0:T(8,128)(2,1)S(1)} %get-tuple-element.32), channel_id=1, source_target_pairs={{0,15},{1,0},{2,1},{3,2},{4,3},{5,4},{6,5},{7,6},{8,7},{9,8},{10,9... | collective-permute-start | bytes 98312 | tf_op jit(solution)/shard_map/ppermute | solution.py:267
  7.1 0.0 collective-permute-start.2
  7.1 0.3 %collective-permute-start.1 = (f32[8,128]{1,0:T(8,128)S(1)}, f32[8,128]{1,0:T(8,128)S(1)}, u32[]{:S(2)}, u32[]{:S(2)}) collective-permute-start(f32[8,128]{1,0:T(8,128)S(1)} %get-tuple-element.34), channel_id=1, source_target_pairs={{0,4},{1,5},{2,6},{3,7},{4,0},{5,1},{6,2},{7,3},{8,12},{9,13},{10,... | collective-permute-start | bytes 12296 | tf_op jit(solution)/shard_map/ppermute | solution.py:277
  7.4 2.1 %lookup.1 = (f32[4,8,128,128]{3,2,1,0:T(8,128)S(1)}, f32[8,128,128]{2,1,0:T(8,128)S(1)}, f32[128,128]{1,0:T(8,128)S(1)}) custom-call(f32[2,8,128]{2,1,0:T(8,128)S(1)} %get-tuple-element.20.knots_ref, bf16[256,256]{1,0:T(8,128)(2,1)S(1)} %get-tuple-element.21.pick_ref, f32[8,144,128]{2,1,0:T(8,128)S(1)} %get-tuple-element.22.s_ref, ...), custom_call_target="tpu_custom_call" | custom-call | flops 7864320 | bytes 3670016 | tf_op jit(solution)/shard_map/lookup/pallas_call | solution.py:279
  9.5 0.0 collective-permute-done.2.swap0_ref
  9.5 1.2 %collective-permute-done.1.swap1_ref = f32[8,128]{1,0:T(8,128)S(1)} collective-permute-done((f32[8,128]{1,0:T(8,128)S(1)}, f32[8,128]{1,0:T(8,128)S(1)}, u32[]{:S(2)}, u32[]{:S(2)}) %collective-permute-start.1) | collective-permute-done | bytes 4128 | tf_op jit(solution)/shard_map/ppermute | solution.py:277
  10.7 0.0 collective-permute-done.before_ref
  10.7 0.5 %most.1 = (f32[16,4,8,128]{3,2,1,0:T(8,128)S(1)}, f32[128,128]{1,0:T(8,128)S(1)}) custom-call(f32[4,8,128,128]{3,2,1,0:T(8,128)S(1)} %get-tuple-element.24.value_ref, f32[8,128,128]{2,1,0:T(8,128)S(1)} %get-tuple-element.25.part_ref, f32[128,128]{1,0:T(8,128)S(1)} %get-tuple-element.26.edge_ref, f32[8,144,128]{2,1,0:T(8,128)S(1)} %get-tuple-element.22.s_ref, ...), custom_call_target="tpu_custom_call" | custom-call | tf_op jit(solution)/shard_map/most/pallas_call | solution.py:288
  11.2 0.0 collective-permute-done.3.after_ref
  11.2 0.2 last.1
  11.4 12.2 %all_to_all.5.slab_ref = s16[16,2,16,128]{3,2,1,0:T(8,128)(2,1)S(1)} all-to-all(s16[16,2,16,128]{3,2,1,0:T(8,128)(2,1)S(1)} %last.1), channel_id=1, replica_groups=mesh['cols'=8,'depth'=16] {'depth'}, dimensions={0} | all-to-all | bytes 262144 | tf_op jit(solution)/shard_map/all_to_all | solution.py:303
  23.5 0.7 %combine.1 = f32[4,8,128]{2,1,0:T(8,128)} custom-call(f32[8,128]{1,0:T(8,128)S(1)} %get-tuple-element.19.scale_ref, s16[16,2,16,128]{3,2,1,0:T(8,128)(2,1)S(1)} %all_to_all.5.slab_ref), custom_call_target="tpu_custom_call" | custom-call | tf_op jit(solution)/shard_map/combine/pallas_call | solution.py:304
  (1 shorter events, 0.0 us)
Async XLA Ops:
  1.6 9.1 %collective-permute-start = (s16[128,128]{1,0:T(8,128)(2,1)S(1)}, s16[128,128]{1,0:T(8,128)(2,1)S(1)}, u32[]{:S(2)}, u32[]{:S(2)}) collective-permute-start(s16[128,128]{1,0:T(8,128)(2,1)S(1)} %get-tuple-element.27), channel_id=1, source_target_pairs={{0,1},{1,2},{2,3},{3,4},{4,5},{5,6},{6,7},{7,8},{8,9},{9,10},{10,1... | collective-permute-start | bytes 98312 | tf_op jit(solution)/shard_map/ppermute | solution.py:268
  3.4 7.8 %collective-permute-start.3 = (s16[128,128]{1,0:T(8,128)(2,1)S(1)}, s16[128,128]{1,0:T(8,128)(2,1)S(1)}, u32[]{:S(2)}, u32[]{:S(2)}) collective-permute-start(s16[128,128]{1,0:T(8,128)(2,1)S(1)} %get-tuple-element.32), channel_id=1, source_target_pairs={{0,15},{1,0},{2,1},{3,2},{4,3},{5,4},{6,5},{7,6},{8,7},{9,8},{10,9... | collective-permute-start | bytes 98312 | tf_op jit(solution)/shard_map/ppermute | solution.py:267
  7.1 2.4 %collective-permute-start.2 = (f32[8,128]{1,0:T(8,128)S(1)}, f32[8,128]{1,0:T(8,128)S(1)}, u32[]{:S(2)}, u32[]{:S(2)}) collective-permute-start(f32[8,128]{1,0:T(8,128)S(1)} %get-tuple-element.33), channel_id=1, source_target_pairs={{0,16},{16,0},{32,48},{48,32},{64,80},{80,64},{96,112},{112,96},{1... | collective-permute-start | bytes 12296 | tf_op jit(solution)/shard_map/ppermute | solution.py:276
  7.1 3.6 %collective-permute-start.1 = (f32[8,128]{1,0:T(8,128)S(1)}, f32[8,128]{1,0:T(8,128)S(1)}, u32[]{:S(2)}, u32[]{:S(2)}) collective-permute-start(f32[8,128]{1,0:T(8,128)S(1)} %get-tuple-element.34), channel_id=1, source_target_pairs={{0,4},{1,5},{2,6},{3,7},{4,0},{5,1},{6,2},{7,3},{8,12},{9,13},{10,... | collective-permute-start | bytes 12296 | tf_op jit(solution)/shard_map/ppermute | solution.py:277

commit v10 on v9

--- a/solution.py
+++ b/solution.py
@@ -26,7 +26,7 @@
     return root * root * scale
 
 
-def strength_kernel(step, q_ref, lab_ref, tab_ref, s_ref, first_ref, last_ref, colfirst_ref, collast_ref, lab_here, knots_ref, scale_ref, pick_ref, q_here, sems, tab_here, rows_tab, edge, edge_t):
+def strength_kernel(step, q_ref, lab_ref, tab_ref, s_ref, first_ref, last_ref, inner_ref, outer_ref, lab_here, knots_ref, scale_ref, pick_ref, q_here, sems, tab_here, rows_tab, edge, edge_t):
     _, nz, rows, lanes = q_here.shape
     tab_copy = pltpu.make_async_copy(tab_ref, tab_here, sems.at[CHUNKS])
     tab_copy.start()
@@ -90,8 +90,9 @@
 
         lax.fori_loop(0, rows // BLOCK, block, 0)
     edge_t[...] = edge[...].T
-    collast_ref[...] = edge_t[pl.ds(0, nz, stride=2), :]
-    colfirst_ref[...] = edge_t[pl.ds(1, nz, stride=2), :]
+    odd = lax.axis_index("cols") % 2
+    inner_ref[...] = edge_t[pl.ds(odd, nz, stride=2), :]
+    outer_ref[...] = edge_t[pl.ds(1 - odd, nz, stride=2), :]
     lab_copy.wait()
 
 
@@ -137,7 +138,7 @@
             below, here = here, above
         return carry
 
-    lax.fori_loop(0, rows // SUB, block, 0, unroll=4)
+    lax.fori_loop(0, rows // SUB, block, 0, unroll=16)
 
 
 def most_kernel(step, value_ref, part_ref, edge_ref, s_ref, before_ref, swap1_ref, swap0_ref,
@@ -242,7 +243,7 @@
     plane = pltpu.VMEM((rows, lanes), jnp.float32)
     nlab, nchan, nbins = tables.shape
     far = lambda array: pltpu.with_memory_space_constraint(array, pltpu.HBM)
-    s, first, last, colfirst, collast, labels, knots, scale, pick = pl.pallas_call(
+    s, first, last, to_inner, to_outer, labels, knots, scale, pick = pl.pallas_call(
         functools.partial(strength_kernel, step),
         in_specs=[pl.BlockSpec(memory_space=pltpu.HBM)] * 3,
         out_shape=[
@@ -266,15 +267,14 @@
     down = lambda n: [(i, (i - 1) % n) for i in range(n)]
     after = lax.ppermute(first, "depth", down(groups))
     before = lax.ppermute(last, "depth", up(groups))
-    c_odd = lax.axis_index("cols") % 2 == 1
     inner = [(i, i ^ 1) for i in range(across)]
     outer = []
     for i in range(across):
         j = ((i + 1) ^ 1) - 1
         for g in range(groups):
             outer.append((i * groups + g, j * groups + g if 0 <= j < across else i * groups + (g ^ groups // 4)))
-    swap0 = lax.ppermute(jnp.where(c_odd, colfirst, collast), "cols", inner)
-    swap1 = lax.ppermute(jnp.where(c_odd, collast, colfirst), ("cols", "depth"), outer)
+    swap0 = lax.ppermute(to_inner, "cols", inner)
+    swap1 = lax.ppermute(to_outer, ("cols", "depth"), outer)
 
     value, part, edge = pl.pallas_call(
         functools.partial(lookup_kernel, nbins),

time: 24.4 us -> 24.4 us (level)
  starting transfers between devices: 5.78 us -> 7.53 us
  waiting for transfers between devices: 1.16 us -> 0.01 us
  Pallas kernels: 5.07 us -> 4.64 us
    ppermute x2, starting transfers between devices: 0.34 us -> 2.09 us  [the longest x1 1.75 us: on_device(): swap0 = lax.ppermute(to_inner, 'cols', inner)]
    ppermute x2, waiting for transfers between devices: 1.16 us -> 0.01 us  [the longest x1 0.01 us: on_device(): swap1 = lax.ppermute(to_outer, ('cols', 'depth'), outer)]
    pallas_call x1, Pallas kernels: 2.1 us -> 1.66 us  [on_device(): pl.pallas_call(functools.partial(lookup_kernel, nbins), out_shape=[f32(nc...]
  transfers between devices with their start and end apart: 4 -> 4, of which waited for: 1 -> 0; matrix products, arithmetic and copies ran while one was open for 0% -> 0% of each run, Pallas kernels for 11% -> 9%
where the time goes in v10:
time: 24.4 us; the launch traced here: 24.2 us
  blocking collectives  12 us (49%)
  starting transfers between devices  7.53 us (31%)
  Pallas kernels  4.64 us (19%)
    all_to_all x1, blocking collectives, on_device(): mine = lax.all_to_all(slabs, 'depth', 0, 0)  12 us
    ppermute x1, starting transfers between devices, on_device(): after = lax.ppermute(first, 'depth', down(groups))  3.71 us
    ppermute x1, starting transfers between devices, on_device(): swap0 = lax.ppermute(to_inner, 'cols', inner)  1.75 us
    ppermute x1, starting transfers between devices, on_device(): before = lax.ppermute(last, 'depth', up(groups))  1.73 us
    pallas_call x1, Pallas kernels, on_device(): pl.pallas_call(functools.partial(lookup_kernel, nbins), out_shape=[f32(nc...  1.66 us
    pallas_call x1, Pallas kernels, on_device(): pl.pallas_call(functools.partial(strength_kernel, step), in_specs=[pl.Blo...  1.62 us
    pallas_call x1, Pallas kernels, on_device(): pl.pallas_call(combine_kernel, out_shape=f32(4, SUB, lanes), compiler_par...  0.68 us
  transfers between devices with their start and end apart: 4, of which 0 were waited for; matrix products, arithmetic and copies ran while one was open for 0% of the time, Pallas kernels for 9%

profile of v10, /device:TPU:0, one launch (start us, length us, event | category | flops | bytes accessed | tf_op | source)
XLA Modules:
  0.0 24.2 jit_solution(16039393207860551703)
XLA Ops:
  0.0 1.6 %strength.1 = (f32[8,144,128]{2,1,0:T(8,128)S(1)}, s16[128,128]{1,0:T(8,128)(2,1)S(1)}, s16[128,128]{1,0:T(8,128)(2,1)S(1)}, f32[8,128]{1,0:T(8,128)S(1)}, f32[8...) custom-call(bf16[5,8,128,128]{3,2,1,0:T(8,128)(2,1)} %q_ref.1, ...), custom_call_target="tpu_custom_call" | custom-call | tf_op jit(solution)/shard_map/strength/pallas_call | solution.py:246
  1.6 1.7 %collective-permute-start = (s16[128,128]{1,0:T(8,128)(2,1)S(1)}, s16[128,128]{1,0:T(8,128)(2,1)S(1)}, u32[]{:S(2)}, u32[]{:S(2)}) collective-permute-start(s16[128,128]{1,0:T(8,128)(2,1)S(1)} %get-tuple-element.27), channel_id=1, source_target_pairs={{0,1},{1,2},{2,3},{3,4},{4,5},{5,6},{6,7},{7,8},{8,9},{9,10},{10,1... | collective-permute-start | bytes 98312 | tf_op jit(solution)/shard_map/ppermute | solution.py:269
  3.4 3.7 %collective-permute-start.3 = (s16[128,128]{1,0:T(8,128)(2,1)S(1)}, s16[128,128]{1,0:T(8,128)(2,1)S(1)}, u32[]{:S(2)}, u32[]{:S(2)}) collective-permute-start(s16[128,128]{1,0:T(8,128)(2,1)S(1)} %get-tuple-element.32), channel_id=1, source_target_pairs={{0,15},{1,0},{2,1},{3,2},{4,3},{5,4},{6,5},{7,6},{8,7},{9,8},{10,9... | collective-permute-start | bytes 98312 | tf_op jit(solution)/shard_map/ppermute | solution.py:268
  7.1 0.3 %collective-permute-start.1 = (f32[8,128]{1,0:T(8,128)S(1)}, f32[8,128]{1,0:T(8,128)S(1)}, u32[]{:S(2)}, u32[]{:S(2)}) collective-permute-start(f32[8,128]{1,0:T(8,128)S(1)} %get-tuple-element.28), channel_id=1, source_target_pairs={{0,4},{1,5},{2,6},{3,7},{4,0},{5,1},{6,2},{7,3},{8,12},{9,13},{10,... | collective-permute-start | bytes 12296 | tf_op jit(solution)/shard_map/ppermute | solution.py:277
  7.4 1.8 %collective-permute-start.2 = (f32[8,128]{1,0:T(8,128)S(1)}, f32[8,128]{1,0:T(8,128)S(1)}, u32[]{:S(2)}, u32[]{:S(2)}) collective-permute-start(f32[8,128]{1,0:T(8,128)S(1)} %get-tuple-element.29), channel_id=1, source_target_pairs={{0,16},{16,0},{32,48},{48,32},{64,80},{80,64},{96,112},{112,96},{1... | collective-permute-start | bytes 12296 | tf_op jit(solution)/shard_map/ppermute | solution.py:276
  9.2 1.7 %lookup.1 = (f32[4,8,128,128]{3,2,1,0:T(8,128)S(1)}, f32[8,128,128]{2,1,0:T(8,128)S(1)}, f32[128,128]{1,0:T(8,128)S(1)}) custom-call(f32[2,8,128]{2,1,0:T(8,128)S(1)} %get-tuple-element.20.knots_ref, bf16[256,256]{1,0:T(8,128)(2,1)S(1)} %get-tuple-element.21.pick_ref, f32[8,144,128]{2,1,0:T(8,128)S(1)} %get-tuple-element.22.s_ref, ...), custom_call_target="tpu_custom_call" | custom-call | flops 7864320 | bytes 3670016 | tf_op jit(solution)/shard_map/lookup/pallas_call | solution.py:279
  10.8 0.0 collective-permute-done.1.swap1_ref
  10.8 0.0 collective-permute-done.2.swap0_ref
  10.8 0.0 collective-permute-done.before_ref
  10.9 0.5 %most.1 = (f32[16,4,8,128]{3,2,1,0:T(8,128)S(1)}, f32[128,128]{1,0:T(8,128)S(1)}) custom-call(f32[4,8,128,128]{3,2,1,0:T(8,128)S(1)} %get-tuple-element.24.value_ref, f32[8,128,128]{2,1,0:T(8,128)S(1)} %get-tuple-element.25.part_ref, f32[128,128]{1,0:T(8,128)S(1)} %get-tuple-element.26.edge_ref, f32[8,144,128]{2,1,0:T(8,128)S(1)} %get-tuple-element.22.s_ref, ...), custom_call_target="tpu_custom_call" | custom-call | tf_op jit(solution)/shard_map/most/pallas_call | solution.py:288
  11.3 0.0 collective-permute-done.3.after_ref
  11.3 0.2 last.1
  11.6 12.0 %all_to_all.5.slab_ref = s16[16,2,16,128]{3,2,1,0:T(8,128)(2,1)S(1)} all-to-all(s16[16,2,16,128]{3,2,1,0:T(8,128)(2,1)S(1)} %last.1), channel_id=1, replica_groups=mesh['cols'=8,'depth'=16] {'depth'}, dimensions={0} | all-to-all | bytes 262144 | tf_op jit(solution)/shard_map/all_to_all | solution.py:303
  23.5 0.7 %combine.1 = f32[4,8,128]{2,1,0:T(8,128)} custom-call(f32[8,128]{1,0:T(8,128)S(1)} %get-tuple-element.19.scale_ref, s16[16,2,16,128]{3,2,1,0:T(8,128)(2,1)S(1)} %all_to_all.5.slab_ref), custom_call_target="tpu_custom_call" | custom-call | tf_op jit(solution)/shard_map/combine/pallas_call | solution.py:304
Async XLA Ops:
  1.6 9.2 %collective-permute-start = (s16[128,128]{1,0:T(8,128)(2,1)S(1)}, s16[128,128]{1,0:T(8,128)(2,1)S(1)}, u32[]{:S(2)}, u32[]{:S(2)}) collective-permute-start(s16[128,128]{1,0:T(8,128)(2,1)S(1)} %get-tuple-element.27), channel_id=1, source_target_pairs={{0,1},{1,2},{2,3},{3,4},{4,5},{5,6},{6,7},{7,8},{8,9},{9,10},{10,1... | collective-permute-start | bytes 98312 | tf_op jit(solution)/shard_map/ppermute | solution.py:269
  3.4 8.0 %collective-permute-start.3 = (s16[128,128]{1,0:T(8,128)(2,1)S(1)}, s16[128,128]{1,0:T(8,128)(2,1)S(1)}, u32[]{:S(2)}, u32[]{:S(2)}) collective-permute-start(s16[128,128]{1,0:T(8,128)(2,1)S(1)} %get-tuple-element.32), channel_id=1, source_target_pairs={{0,15},{1,0},{2,1},{3,2},{4,3},{5,4},{6,5},{7,6},{8,7},{9,8},{10,9... | collective-permute-start | bytes 98312 | tf_op jit(solution)/shard_map/ppermute | solution.py:268
  7.1 3.8 %collective-permute-start.1 = (f32[8,128]{1,0:T(8,128)S(1)}, f32[8,128]{1,0:T(8,128)S(1)}, u32[]{:S(2)}, u32[]{:S(2)}) collective-permute-start(f32[8,128]{1,0:T(8,128)S(1)} %get-tuple-element.28), channel_id=1, source_target_pairs={{0,4},{1,5},{2,6},{3,7},{4,0},{5,1},{6,2},{7,3},{8,12},{9,13},{10,... | collective-permute-start | bytes 12296 | tf_op jit(solution)/shard_map/ppermute | solution.py:277
  7.4 3.4 %collective-permute-start.2 = (f32[8,128]{1,0:T(8,128)S(1)}, f32[8,128]{1,0:T(8,128)S(1)}, u32[]{:S(2)}, u32[]{:S(2)}) collective-permute-start(f32[8,128]{1,0:T(8,128)S(1)} %get-tuple-element.29), channel_id=1, source_target_pairs={{0,16},{16,0},{32,48},{48,32},{64,80},{80,64},{96,112},{112,96},{1... | collective-permute-start | bytes 12296 | tf_op jit(solution)/shard_map/ppermute | solution.py:276

commit v11 on v10

--- a/solution.py
+++ b/solution.py
@@ -16,8 +16,8 @@
 STRENGTH_MAX = 3.0 * 6.0 * 2.5 * 2.5 * MARGIN
 
 
-def encode(value, scale):
-    level = jnp.sqrt(jnp.clip(value / scale, 0.0, 1.0)) * LEVELS + 0.5
+def encode(value, inverse):
+    level = jnp.sqrt(jnp.clip(value * inverse, 0.0, 1.0)) * LEVELS + 0.5
     return level.astype(jnp.int32) - MIDDLE
 
 
@@ -80,9 +80,9 @@
                 s = 3.0 * (q[0] * q[0] + q[3] * q[3] + q[0] * q[3] + q[1] * q[1] + q[2] * q[2] + q[4] * q[4])
                 s_ref[z, pl.ds(r0 + PAD, BLOCK), :] = s
                 if z == 0:
-                    first_ref[pl.ds(r0, BLOCK), :] = encode(s, STRENGTH_MAX).astype(jnp.int16)
+                    first_ref[pl.ds(r0, BLOCK), :] = encode(s, 1.0 / STRENGTH_MAX).astype(jnp.int16)
                 if z == nz - 1:
-                    last_ref[pl.ds(r0, BLOCK), :] = encode(s, STRENGTH_MAX).astype(jnp.int16)
+                    last_ref[pl.ds(r0, BLOCK), :] = encode(s, 1.0 / STRENGTH_MAX).astype(jnp.int16)
                 turned = pltpu.roll(s, 2 * z + 1, 1)
                 packed = jnp.where(lane >> 1 == z, turned, packed)
             edge[pl.ds(r0, BLOCK), :] = packed
@@ -194,7 +194,8 @@
     _, nz, rows, lanes = value_ref.shape
     has_after = (lax.axis_index("depth") < lax.axis_size("depth") - 1).astype(jnp.float32)
     above_here[...] = decode(after_ref[...].astype(jnp.int32), STRENGTH_MAX) * has_after
-    scale = [jnp.broadcast_to(scale_ref[k:k + 1, :], (SUB, lanes)) for k in range(4)]
+    bound = 1.0 / scale_ref[...]
+    inverse = [jnp.broadcast_to(bound[k:k + 1, :], (SUB, lanes)) for k in range(4)]
 
     def block(i, carry):
         r0 = pl.multiple_of(i * SUB, SUB)
@@ -206,7 +207,7 @@
         passed = transmit * jnp.exp(-step * extinction)
         weight = transmit - passed
         colors = [state_ref[i, chan] + weight * value_ref[chan, nz - 1, at, :] for chan in range(3)]
-        sent = [encode(v, scale[k]) for k, v in enumerate(colors + [1.0 - passed])]
+        sent = [encode(v, inverse[k]) for k, v in enumerate(colors + [1.0 - passed])]
         out_ref[i, 0] = jnp.concatenate(sent[:2], axis=0).astype(jnp.int16)
         out_ref[i, 1] = jnp.concatenate(sent[2:], axis=0).astype(jnp.int16)
         return carry

time: 24.4 us -> 24.4 us (level)
  no operation moved by 1% of the time
where the time goes in v11:
time: 24.4 us; the launch traced here: 24.2 us
  blocking collectives  12 us (49%)
  starting transfers between devices  7.53 us (31%)
  Pallas kernels  4.64 us (19%)
    all_to_all x1, blocking collectives, on_device(): mine = lax.all_to_all(slabs, 'depth', 0, 0)  12 us
    ppermute x1, starting transfers between devices, on_device(): after = lax.ppermute(first, 'depth', down(groups))  3.71 us
    ppermute x1, starting transfers between devices, on_device(): swap0 = lax.ppermute(to_inner, 'cols', inner)  1.75 us
    ppermute x1, starting transfers between devices, on_device(): before = lax.ppermute(last, 'depth', up(groups))  1.73 us
    pallas_call x1, Pallas kernels, on_device(): pl.pallas_call(functools.partial(lookup_kernel, nbins), out_shape=[f32(nc...  1.66 us
    pallas_call x1, Pallas kernels, on_device(): pl.pallas_call(functools.partial(strength_kernel, step), in_specs=[pl.Blo...  1.62 us
    pallas_call x1, Pallas kernels, on_device(): pl.pallas_call(combine_kernel, out_shape=f32(4, SUB, lanes), compiler_par...  0.68 us
  transfers between devices with their start and end apart: 4, of which 0 were waited for; matrix products, arithmetic and copies ran while one was open for 0% of the time, Pallas kernels for 9%

profile of v11, /device:TPU:0, one launch (start us, length us, event | category | flops | bytes accessed | tf_op | source)
XLA Modules:
  0.0 24.2 jit_solution(566009948061032959)
XLA Ops:
  0.0 1.6 %strength.1 = (f32[8,144,128]{2,1,0:T(8,128)S(1)}, s16[128,128]{1,0:T(8,128)(2,1)S(1)}, s16[128,128]{1,0:T(8,128)(2,1)S(1)}, f32[8,128]{1,0:T(8,128)S(1)}, f32[8...) custom-call(bf16[5,8,128,128]{3,2,1,0:T(8,128)(2,1)} %q_ref.1, ...), custom_call_target="tpu_custom_call" | custom-call | tf_op jit(solution)/shard_map/strength/pallas_call | solution.py:247
  1.6 1.7 %collective-permute-start = (s16[128,128]{1,0:T(8,128)(2,1)S(1)}, s16[128,128]{1,0:T(8,128)(2,1)S(1)}, u32[]{:S(2)}, u32[]{:S(2)}) collective-permute-start(s16[128,128]{1,0:T(8,128)(2,1)S(1)} %get-tuple-element.27), channel_id=1, source_target_pairs={{0,1},{1,2},{2,3},{3,4},{4,5},{5,6},{6,7},{7,8},{8,9},{9,10},{10,1... | collective-permute-start | bytes 98312 | tf_op jit(solution)/shard_map/ppermute | solution.py:270
  3.4 3.7 %collective-permute-start.3 = (s16[128,128]{1,0:T(8,128)(2,1)S(1)}, s16[128,128]{1,0:T(8,128)(2,1)S(1)}, u32[]{:S(2)}, u32[]{:S(2)}) collective-permute-start(s16[128,128]{1,0:T(8,128)(2,1)S(1)} %get-tuple-element.32), channel_id=1, source_target_pairs={{0,15},{1,0},{2,1},{3,2},{4,3},{5,4},{6,5},{7,6},{8,7},{9,8},{10,9... | collective-permute-start | bytes 98312 | tf_op jit(solution)/shard_map/ppermute | solution.py:269
  7.1 0.3 %collective-permute-start.1 = (f32[8,128]{1,0:T(8,128)S(1)}, f32[8,128]{1,0:T(8,128)S(1)}, u32[]{:S(2)}, u32[]{:S(2)}) collective-permute-start(f32[8,128]{1,0:T(8,128)S(1)} %get-tuple-element.28), channel_id=1, source_target_pairs={{0,4},{1,5},{2,6},{3,7},{4,0},{5,1},{6,2},{7,3},{8,12},{9,13},{10,... | collective-permute-start | bytes 12296 | tf_op jit(solution)/shard_map/ppermute | solution.py:278
  7.4 1.8 %collective-permute-start.2 = (f32[8,128]{1,0:T(8,128)S(1)}, f32[8,128]{1,0:T(8,128)S(1)}, u32[]{:S(2)}, u32[]{:S(2)}) collective-permute-start(f32[8,128]{1,0:T(8,128)S(1)} %get-tuple-element.29), channel_id=1, source_target_pairs={{0,16},{16,0},{32,48},{48,32},{64,80},{80,64},{96,112},{112,96},{1... | collective-permute-start | bytes 12296 | tf_op jit(solution)/shard_map/ppermute | solution.py:277
  9.2 1.7 %lookup.1 = (f32[4,8,128,128]{3,2,1,0:T(8,128)S(1)}, f32[8,128,128]{2,1,0:T(8,128)S(1)}, f32[128,128]{1,0:T(8,128)S(1)}) custom-call(f32[2,8,128]{2,1,0:T(8,128)S(1)} %get-tuple-element.20.knots_ref, bf16[256,256]{1,0:T(8,128)(2,1)S(1)} %get-tuple-element.21.pick_ref, f32[8,144,128]{2,1,0:T(8,128)S(1)} %get-tuple-element.22.s_ref, ...), custom_call_target="tpu_custom_call" | custom-call | flops 7864320 | bytes 3670016 | tf_op jit(solution)/shard_map/lookup/pallas_call | solution.py:280
  10.8 0.0 collective-permute-done.1.swap1_ref
  10.8 0.0 collective-permute-done.2.swap0_ref
  10.8 0.0 collective-permute-done.before_ref
  10.9 0.5 %most.1 = (f32[16,4,8,128]{3,2,1,0:T(8,128)S(1)}, f32[128,128]{1,0:T(8,128)S(1)}) custom-call(f32[4,8,128,128]{3,2,1,0:T(8,128)S(1)} %get-tuple-element.24.value_ref, f32[8,128,128]{2,1,0:T(8,128)S(1)} %get-tuple-element.25.part_ref, f32[128,128]{1,0:T(8,128)S(1)} %get-tuple-element.26.edge_ref, f32[8,144,128]{2,1,0:T(8,128)S(1)} %get-tuple-element.22.s_ref, ...), custom_call_target="tpu_custom_call" | custom-call | tf_op jit(solution)/shard_map/most/pallas_call | solution.py:289
  11.3 0.0 collective-permute-done.3.after_ref
  11.3 0.2 last.1
  11.6 12.0 %all_to_all.5.slab_ref = s16[16,2,16,128]{3,2,1,0:T(8,128)(2,1)S(1)} all-to-all(s16[16,2,16,128]{3,2,1,0:T(8,128)(2,1)S(1)} %last.1), channel_id=1, replica_groups=mesh['cols'=8,'depth'=16] {'depth'}, dimensions={0} | all-to-all | bytes 262144 | tf_op jit(solution)/shard_map/all_to_all | solution.py:304
  23.5 0.7 %combine.1 = f32[4,8,128]{2,1,0:T(8,128)} custom-call(f32[8,128]{1,0:T(8,128)S(1)} %get-tuple-element.19.scale_ref, s16[16,2,16,128]{3,2,1,0:T(8,128)(2,1)S(1)} %all_to_all.5.slab_ref), custom_call_target="tpu_custom_call" | custom-call | tf_op jit(solution)/shard_map/combine/pallas_call | solution.py:305
Async XLA Ops:
  1.6 9.2 %collective-permute-start = (s16[128,128]{1,0:T(8,128)(2,1)S(1)}, s16[128,128]{1,0:T(8,128)(2,1)S(1)}, u32[]{:S(2)}, u32[]{:S(2)}) collective-permute-start(s16[128,128]{1,0:T(8,128)(2,1)S(1)} %get-tuple-element.27), channel_id=1, source_target_pairs={{0,1},{1,2},{2,3},{3,4},{4,5},{5,6},{6,7},{7,8},{8,9},{9,10},{10,1... | collective-permute-start | bytes 98312 | tf_op jit(solution)/shard_map/ppermute | solution.py:270
  3.4 8.0 %collective-permute-start.3 = (s16[128,128]{1,0:T(8,128)(2,1)S(1)}, s16[128,128]{1,0:T(8,128)(2,1)S(1)}, u32[]{:S(2)}, u32[]{:S(2)}) collective-permute-start(s16[128,128]{1,0:T(8,128)(2,1)S(1)} %get-tuple-element.32), channel_id=1, source_target_pairs={{0,15},{1,0},{2,1},{3,2},{4,3},{5,4},{6,5},{7,6},{8,7},{9,8},{10,9... | collective-permute-start | bytes 98312 | tf_op jit(solution)/shard_map/ppermute | solution.py:269
  7.1 3.8 %collective-permute-start.1 = (f32[8,128]{1,0:T(8,128)S(1)}, f32[8,128]{1,0:T(8,128)S(1)}, u32[]{:S(2)}, u32[]{:S(2)}) collective-permute-start(f32[8,128]{1,0:T(8,128)S(1)} %get-tuple-element.28), channel_id=1, source_target_pairs={{0,4},{1,5},{2,6},{3,7},{4,0},{5,1},{6,2},{7,3},{8,12},{9,13},{10,... | collective-permute-start | bytes 12296 | tf_op jit(solution)/shard_map/ppermute | solution.py:278
  7.4 3.4 %collective-permute-start.2 = (f32[8,128]{1,0:T(8,128)S(1)}, f32[8,128]{1,0:T(8,128)S(1)}, u32[]{:S(2)}, u32[]{:S(2)}) collective-permute-start(f32[8,128]{1,0:T(8,128)S(1)} %get-tuple-element.29), channel_id=1, source_target_pairs={{0,16},{16,0},{32,48},{48,32},{64,80},{80,64},{96,112},{112,96},{1... | collective-permute-start | bytes 12296 | tf_op jit(solution)/shard_map/ppermute | solution.py:277
